TPU v7x, 32 devices: a whole 2x2x4 slice. The times are simulated.
32 devices in a mesh: wide: 16 (over z, x, core), narrow: 2 (over y).
Axes of the slice: x: 2, y: 2, z: 4, core: 2. Of those that a mesh axis runs over, the one named last changes fastest.
Arguments:
- sensitivity: float32 [6, 262144], P(None, ('wide', 'narrow')), may hold values from -0.18 to 0.18
- vol_coord: float32 [3, 262144], P(None, ('wide', 'narrow')), may hold values from 0 to 1
- ctl_coord: float32 [3, 32768], replicated, may hold values from 0 to 1
- pair_list: int32 [2, 16384], P(None, ('wide', 'narrow')), may hold values from 0 to 255, as said below
- pair_count: int32 [32], P(('wide', 'narrow')), may hold values from 85 to 512, as said below
- inverse: bfloat16 [32768, 32768], P('wide', 'narrow'), may hold values from -0.046875 to 0.046875
Outputs:
- gradient: float32 [6, 32768], P(None, ('narrow', 'wide'))
Inputs may be any that keep to these rules, and one draw needn't show every extreme that they name: `pair_list`: row 0 lies in 0 to 63. The first slot of device d names control tile ((d + 16) % 32) * 8. Row 1 of device d's other slots lies in a band of 16 control tiles that starts at d * 8 and wraps past the last tile. Slots at or past their device's count are not used. `pair_count`: some device has exactly 512 used slots in every draw.
All inputs are finite; a program needn't handle non-finite values.
Results may differ from a plain program's by a relative error of at most 0.0029.
Values may be sent and summed in bfloat16 or wider, within the bound.
No kernel may reach another device: no remote copies, remote signals or barrier semaphores. Data moves between devices by JAX's collectives and lax.ppermute only.
A program may use at most 128 MiB of HBM per device.

v0:
```python
import math

import jax
import jax.numpy as jnp
from jax import lax
from jax.sharding import PartitionSpec as P

CT = 128
VT = 128
PAIR_MAX = 512


def wendland_terms(sens_tile, node_tile, point_tile):
    squared = (node_tile[0][:, :, None] - point_tile[0][:, None, :]) ** 2
    for axis_num in (1, 2):
        squared = (
            squared + (node_tile[axis_num][:, :, None] - point_tile[axis_num][:, None, :]) ** 2
        )
    radius = jnp.sqrt(squared)
    inside = jnp.maximum(1.0 - radius, 0.0)
    kernel = inside * inside * inside * inside * (4.0 * radius + 1.0)
    return jnp.einsum("cbv,bvt->cbt", sens_tile, kernel, precision=lax.Precision.HIGHEST)


def accumulate(acc_sum, sens_tiles, pos_tiles, point_tiles, vol_ids, ctl_ids, live):
    sens_tile = jnp.take(sens_tiles, vol_ids, axis=1) * live[None, :, None]
    node_tile = jnp.take(pos_tiles, vol_ids, axis=1)
    point_tile = jnp.take(point_tiles, ctl_ids, axis=1)
    terms = wendland_terms(sens_tile, node_tile, point_tile)
    return acc_sum.at[:, ctl_ids, :].add(terms)


def local(sensitivity, vol_coord, ctl_coord, pair_list, pair_count, inverse):
    components = sensitivity.shape[0]
    point_tiles = ctl_coord.reshape(3, -1, CT)
    pblock = math.gcd(64, PAIR_MAX)
    offsets = jnp.arange(pblock, dtype=jnp.int32)
    zeros = jnp.zeros((components, point_tiles.shape[1], CT), jnp.float32)
    sens_tiles = sensitivity.reshape(components, -1, VT)
    pos_tiles = vol_coord.reshape(3, -1, VT)
    own_count = pair_count[0]

    def own_step(block_id, acc_sum):
        first_slot = block_id * pblock
        listed = lax.dynamic_slice_in_dim(pair_list, first_slot, pblock, 1)
        live = (first_slot + offsets < own_count).astype(jnp.float32)
        return accumulate(acc_sum, sens_tiles, pos_tiles, point_tiles, listed[0], listed[1], live)

    nblocks = (own_count + pblock - 1) // pblock
    loads = lax.fori_loop(0, nblocks, own_step, zeros)
    loads = loads.reshape(components, -1)
    row_count = inverse.shape[0]
    whole = lax.psum(loads, ("wide", "narrow"))
    row_loads = lax.dynamic_slice_in_dim(
        whole, lax.axis_index("wide") * row_count, row_count, 1
    ).astype(jnp.bfloat16)
    col_terms = jnp.dot(row_loads, inverse, preferred_element_type=jnp.float32)
    return lax.psum_scatter(col_terms, "wide", scatter_dimension=1, tiled=True)


def solution(mesh):
    return jax.shard_map(
        local,
        mesh=mesh,
        in_specs=(
            P(None, ("wide", "narrow")),
            P(None, ("wide", "narrow")),
            P(),
            P(None, ("wide", "narrow")),
            P(("wide", "narrow")),
            P("wide", "narrow"),
        ),
        out_specs=P(None, ("narrow", "wide")),
        check_vma=False,
    )
```

profile of v0, /device:TPU:0, one launch (start us, length us, event | category | flops | bytes accessed | tf_op | source)
XLA Modules:
  0.0 293.8 jit_solution(3916240992771863505)
XLA Ops:
  6.5 0.0 reduce-scatter.2.cloned.1.call-start
  7.2 0.1 broadcast_in_dim.33
  7.3 38.3 %while.11 = (s32[]{:T(128)}, f32[6,256,128]{2,0,1:T(8,128)S(1)}, s32[]{:T(128)}, s32[2,512]{1,0:T(2,128)}, f32[3,64,128]{2,0,1:T(4,128)}, /*index=5*/f32[3,256,1...) while((s32[]{:T(128)}, f32[6,256,128]{2,0,1:T(8,128)S(1)}, ...), condition=%wide.region_2.3_spmd.clone, body=%wide.region_0.2_spmd.clone.sunk | while | flops 92474696 | bytes 2765807 | solution.py:50
  7.3 0.8 constant_dynamic-slice_fusion.2
  8.1 1.6 gather_fusion.1
  9.7 0.7 compare_and_fusion.3
  10.3 0.1 select_bitcast_fusion.5
  10.5 0.1 fusion.54
  10.5 1.7 gather_fusion
  12.2 0.1 select_bitcast_fusion.4
  12.4 0.1 fusion.53
  12.5 1.5 gather_fusion.2
  14.0 9.6 %fusion.55 = f32[64,6,128]{2,1,0:T(8,128)S(1)} fusion(f32[64,128]{1,0:T(8,128)S(1)} %bitcast.63, f32[64,128]{1,0:T(8,128)S(1)} %bitcast.60, f32[64,128]{1,0:T(8,128)S(1)} %bitcast.64, f32[64,128]{1,0:T(8,128)S(1)} %bitcast.61, f32[64,128]{1,0:T(8,128)S(1)} %bitcast.62, f32[64,128]{1,0:T(8,128)S(1)} %bitcast.59, f32[64,6,128]{2,1,0:T(8,128)S(1)} %gather_fusion.2, ...), kind=kOutput, calls=%fused_computation.7.clone.1 | convolution fusion | flops 92372992 | bytes 590144 | tf_op jit(solution)/shard_map/while/body/cbv,bvt->cbt/dot_general | solution.py:22
  23.6 2.8 scatter_fusion
  26.4 0.8 constant_dynamic-slice_fusion.2
  27.2 1.6 gather_fusion.1
  28.8 0.7 compare_and_fusion.3
  29.4 0.1 select_bitcast_fusion.5
  29.6 0.1 fusion.54
  29.7 1.7 gather_fusion
  31.4 0.1 select_bitcast_fusion.4
  31.5 0.1 fusion.53
  31.6 1.5 gather_fusion.2
  33.1 9.6 %fusion.55 = f32[64,6,128]{2,1,0:T(8,128)S(1)} fusion(f32[64,128]{1,0:T(8,128)S(1)} %bitcast.63, f32[64,128]{1,0:T(8,128)S(1)} %bitcast.60, f32[64,128]{1,0:T(8,128)S(1)} %bitcast.64, f32[64,128]{1,0:T(8,128)S(1)} %bitcast.61, f32[64,128]{1,0:T(8,128)S(1)} %bitcast.62, f32[64,128]{1,0:T(8,128)S(1)} %bitcast.59, f32[64,6,128]{2,1,0:T(8,128)S(1)} %gather_fusion.2, ...), kind=kOutput, calls=%fused_computation.7.clone.1 | convolution fusion | flops 92372992 | bytes 590144 | tf_op jit(solution)/shard_map/while/body/cbv,bvt->cbt/dot_general | solution.py:22
  42.8 2.8 scatter_fusion
  45.6 162.8 %all-reduce.1 = bf16[6,32768]{1,0:T(8,128)(2,1)S(1)} all-reduce(f32[6,32768]{1,0:T(8,128)S(1)} %bitcast.56), channel_id=1, replica_groups=mesh['wide'=16,'narrow'=2] {'wide','narrow'}, use_global_device_ids=true, to_apply=%region_3.4 | all-reduce | flops 196608 | bytes 1179648 | tf_op jit(solution)/shard_map/psum | solution.py:53
  208.3 23.4 %fusion.39 = f32[6,16384]{1,0:T(8,128)} fusion(bf16[2048,16384]{1,0:T(8,128)(2,1)} %param.13, bf16[6,32768]{1,0:T(8,128)(2,1)S(1)} %all-reduce.1, s32[]{:T(128)S(6)} %select_n.58), kind=kOutput, calls=%fused_computation.56 | convolution fusion | flops 402653184 | bytes 67534848 | tf_op jit(solution)/shard_map/dot_general | solution.py:57
  231.7 0.0 reduce-scatter.2.cloned.1.call-update
  231.8 55.1 %reduce-scatter.2.cloned.1.call-done = f32[6,1024]{1,0:T(8,128)} async-done(((f32[6,16384]{1,0:T(8,128)}), f32[6,1024]{1,0:T(8,128)}) %reduce-scatter.2.cloned.1.call-update) | async-done | bytes 24592 | tf_op jit(solution)/shard_map/reduce_scatter | solution.py:58
  (4 shorter events, 0.0 us)
Async XLA Ops:
  6.5 280.4 %reduce-scatter.2.cloned.1.call-start = ((), (), s32[]{:S(2)}) async-start(), calls=%async_computation.1 | async-start | bytes 557056 | tf_op jit(solution)/shard_map/reduce_scatter | solution.py:58
Sparse Core Ops, SparseCore 0:
  231.9 54.9 reduce-scatter.1
where the time goes:
time: 295 us; the launch traced here: 294 us
  blocking collectives  163 us (55%)
  waiting for transfers between devices  55.2 us (19%)
  matrix products  42.6 us (14%)
  between operations  14.1 us (5%)
  local copies, waits for them, and re-layouts  11.5 us (4%)
  other arithmetic  7.44 us (3%)
    psum x1, blocking collectives, local(): whole = lax.psum(loads, ('wide', 'narrow'))  163 us
    reduce_scatter x1, waiting for transfers between devices, local(): return lax.psum_scatter(col_terms, 'wide', scatter_dimension=1, tiled=True)  55.1 us
    dot_general x1, matrix products, local(): col_terms = jnp.dot(row_loads, inverse, preferred_element_type=jnp.float32)  23.4 us
    dot_general x2, matrix products, wendland_terms(): jnp.einsum('cbv,bvt->cbt', sens_tile, kernel, precision=lax.Precision.HIG...  19.2 us
  transfers between devices with their start and end apart: 1, of which 1 were waited for; matrix products, arithmetic and copies ran while one was open for 0% of the time, Pallas kernels for 0%

commit v1 on v0

v1 whole, which is shorter than its diff:
```python
import functools

import jax
import jax.numpy as jnp
from jax import lax
from jax.experimental import pallas as pl
from jax.experimental.pallas import tpu as pltpu
from jax.sharding import PartitionSpec as P

CT = 128
VT = 128
BAND = 16
UNROLL = 4
ROWS = 8
DEPTH = 64
MIB = 1 << 20
PIECE = 256
HELD = 4
MORE = 1
SLOTS = 4


def thirds(value):
    high = value.astype(jnp.bfloat16).astype(jnp.float32)
    rest = value - high
    middle = rest.astype(jnp.bfloat16).astype(jnp.float32)
    return high, middle, rest - middle


def features(coords, is_node):
    width = coords.shape[1]
    scaled = 4.0 * coords - 2.0
    norm = scaled[0:1] * scaled[0:1] + scaled[1:2] * scaled[1:2] + scaled[2:3] * scaled[2:3]
    padded = jnp.concatenate([scaled, jnp.zeros((ROWS - 3, width), jnp.float32)], axis=0)
    high, middle, low = thirds(padded)
    row = lax.broadcasted_iota(jnp.int32, (ROWS, width), 0)
    n_high, n_middle, n_low = thirds(jnp.broadcast_to(norm, (ROWS, width)))
    first = 0 if is_node else 3
    norms = jnp.where(
        row == first,
        n_high,
        jnp.where(row == first + 1, n_middle, jnp.where(row == first + 2, n_low, 0.0)),
    )
    ones = jnp.where((row >= 3 - first) & (row < 6 - first), 1.0, 0.0)
    last = norms + ones
    if is_node:
        parts = [high, high, middle, middle, high, low, last]
    else:
        parts = [high, middle, high, middle, low, high]
        parts = [-2.0 * part for part in parts] + [last]
    parts = parts + [jnp.zeros((DEPTH - ROWS * len(parts), width), jnp.float32)]
    return jnp.concatenate(parts, axis=0)


def held_copies(first, inverse_ref, held_refs, sems):
    return [
        pltpu.make_async_copy(
            inverse_ref.at[pl.ds((first + at) * PIECE, PIECE), :], held_ref, sems.at[at]
        )
        for at, held_ref in enumerate(held_refs)
    ]


def pair_kernel(
    geometry,
    held_count,
    list_ref,
    count_ref,
    place_ref,
    sens_ref,
    vol_ref,
    ctl_ref,
    inverse_ref,
    own_ref,
    spill_ref,
    far_ref,
    *rest,
):
    ctiles, tpb, tiles = geometry
    held_refs, rest = rest[:held_count], rest[held_count:]
    nodes, points, weights, loads_ref = rest[:4]
    vtiles = vol_ref.shape[1] // VT
    copies = held_copies(0, inverse_ref, held_refs, rest[4]) if held_count else []
    for copy in copies:
        copy.start()

    first_tile = place_ref[0]
    far_tile = place_ref[1]

    group = 8

    def node_group(group_id, carry):
        begin = pl.multiple_of(group_id * (group * VT), group * VT)
        rows = features(vol_ref[:, pl.ds(begin, group * VT)], True)
        sens = sens_ref[:, pl.ds(begin, group * VT)]
        components = sens.shape[0]
        if components < ROWS:
            sens = jnp.concatenate(
                [sens, jnp.zeros((ROWS - components, group * VT), jnp.float32)], axis=0
            )
        high = sens.astype(jnp.bfloat16).astype(jnp.float32)
        both = jnp.concatenate([high, sens - high], axis=0).astype(jnp.bfloat16)
        for at in range(group):
            cut = slice(at * VT, (at + 1) * VT)
            nodes[group_id * group + at] = rows[:, cut].T.astype(jnp.bfloat16)
            weights[group_id * group + at] = jnp.concatenate([both[:, cut], both[:, cut]], axis=1)
        return carry

    lax.fori_loop(0, vtiles // group, node_group, 0)
    weights[vtiles] = jnp.zeros(weights.shape[1:], jnp.bfloat16)

    def point_tile(tile, carry):
        named = lax.rem(first_tile + tile, ctiles)
        named = jnp.where(tile == tiles, far_tile, named)
        begin = pl.multiple_of(named * CT, CT)
        points[tile] = features(ctl_ref[:, pl.ds(begin, CT)], False).astype(jnp.bfloat16)
        loads_ref[tile] = jnp.zeros((ROWS, CT), jnp.float32)
        return carry

    lax.fori_loop(0, tiles + 1, point_tile, 0)

    count = count_ref[0]

    def pairs_step(step_id, carry):
        results = []
        for at in range(UNROLL):
            slot = step_id * UNROLL + at
            live = slot < count
            volume = jnp.where(live, list_ref[0, slot], 0)
            control = list_ref[1, slot] - first_tile
            control = jnp.where(control < 0, control + ctiles, control)
            control = jnp.where(slot == 0, tiles, control)
            control = jnp.where(live, control, 0)
            squared = jnp.dot(nodes[volume], points[control], preferred_element_type=jnp.float32)
            squared = jnp.maximum(squared, 1e-12)
            radius = squared * lax.rsqrt(squared)
            inside = jnp.maximum(4.0 - radius, 0.0)
            inside = inside * inside
            kernel = inside * inside * (radius + 1.0)
            high = kernel.astype(jnp.bfloat16)
            low = (kernel - high.astype(jnp.float32)).astype(jnp.bfloat16)
            weight = weights[jnp.where(live, volume, vtiles)]
            terms = jnp.dot(
                weight, jnp.concatenate([high, low], axis=0), preferred_element_type=jnp.float32
            )
            results.append((control, terms[:ROWS] + terms[ROWS:]))
        for control, terms in results:
            loads_ref[control] = loads_ref[control] + terms
        return carry

    lax.fori_loop(0, (count + UNROLL - 1) // UNROLL, pairs_step, 0)
    own_ref[...] = loads_ref[:tpb] * (1.0 / 256.0)
    spill_ref[...] = loads_ref[tpb:tiles] * (1.0 / 256.0)
    far_ref[...] = loads_ref[tiles:] * (1.0 / 256.0)
    for copy in copies:
        copy.wait()


def vmem(shape=None):
    return pl.BlockSpec(memory_space=pltpu.VMEM)


def smem():
    return pl.BlockSpec(memory_space=pltpu.SMEM)


def anywhere():
    return pl.BlockSpec(memory_space=pl.ANY)


def pair_stage(geometry, held_count, pair_list, pair_count, place, sens, vol, ctl, inverse):
    ctiles, tpb, tiles = geometry
    vtiles = vol.shape[1] // VT
    columns = inverse.shape[1]
    out_shape = [
        jax.ShapeDtypeStruct((count, ROWS, CT), jnp.float32) for count in (tpb, tiles - tpb, 1)
    ]
    out_specs = [vmem()] * 3
    scratch = [
        pltpu.VMEM((vtiles, VT, DEPTH), jnp.bfloat16),
        pltpu.VMEM((tiles + 1, DEPTH, CT), jnp.bfloat16),
        pltpu.VMEM((vtiles + 1, 2 * ROWS, 2 * VT), jnp.bfloat16),
        pltpu.VMEM((tiles + 1, ROWS, CT), jnp.float32),
    ]
    if held_count:
        out_shape += [pltpu.VMEM((PIECE, columns), inverse.dtype)] * held_count
        out_specs += [vmem()] * held_count
        scratch.append(pltpu.SemaphoreType.DMA((held_count,)))
    return pl.pallas_call(
        functools.partial(pair_kernel, geometry, held_count),
        out_shape=out_shape,
        in_specs=[smem(), smem(), smem(), vmem(), vmem(), vmem(), anywhere()],
        out_specs=out_specs,
        scratch_shapes=scratch,
        compiler_params=pltpu.CompilerParams(vmem_limit_bytes=10 * MIB),
        cost_estimate=pl.CostEstimate(
            flops=512 * 16384 * 400, bytes_accessed=held_count * PIECE * columns * 2, transcendentals=0
        ),
        name="pairs",
    )(pair_list, pair_count, place, sens, vol, ctl, inverse)


def hold_kernel(first, token_ref, inverse_ref, *rest):
    del token_ref
    copies = held_copies(first, inverse_ref, rest[:-1], rest[-1])
    for copy in copies:
        copy.start()
    for copy in copies:
        copy.wait()


def hold_stage(first, count, token, inverse):
    columns = inverse.shape[1]
    return pl.pallas_call(
        functools.partial(hold_kernel, first),
        out_shape=[pltpu.VMEM((PIECE, columns), inverse.dtype)] * count,
        in_specs=[anywhere(), anywhere()],
        out_specs=[vmem()] * count,
        scratch_shapes=[pltpu.SemaphoreType.DMA((count,))],
        compiler_params=pltpu.CompilerParams(vmem_limit_bytes=1 * MIB),
        cost_estimate=pl.CostEstimate(
            flops=0, bytes_accessed=2 * count * PIECE * columns * 2, transcendentals=0
        ),
        name="hold",
    )(token, inverse)


def product_kernel(
    orders,
    offsets,
    place_ref,
    own_ref,
    partner_ref,
    spill_a_ref,
    spill_b_ref,
    far_same_ref,
    far_cross_ref,
    *rest,
):
    held_refs = rest[:-6]
    inverse_ref, send_ref, keep_ref, ring, row_loads, sems = rest[-6:]
    tpb = partner_ref.shape[0]
    spilled = spill_a_ref.shape[0]
    chunks = len(orders)
    columns = inverse_ref.shape[1]
    chunk = columns // chunks
    slots = ring.shape[0]
    streamed = ring.shape[1]
    held = inverse_ref.shape[0] - streamed
    me = place_ref[2]
    even = place_ref[3] == 0

    def column_of(order):
        return pl.multiple_of((me ^ order) * chunk, chunk)

    def fetch(at):
        return pltpu.make_async_copy(
            inverse_ref.at[pl.ds(held, streamed), pl.ds(column_of(orders[at]), chunk)],
            ring.at[at % slots],
            sems.at[at % slots],
        )

    for at in range(slots):
        fetch(at).start()

    for tile in range(tpb):
        total = own_ref[tile] + partner_ref[tile]
        if tile < spilled:
            total = total + jnp.where(even, spill_a_ref[tile], spill_b_ref[tile])
        if tile == offsets[0]:
            total = total + jnp.where(even, far_same_ref[0], far_cross_ref[0])
        if tile == offsets[1]:
            total = total + jnp.where(even, far_cross_ref[0], far_same_ref[0])
        both = jnp.concatenate([total, jnp.zeros_like(total)], axis=0)
        row_loads[:, tile * CT : (tile + 1) * CT] = both.astype(jnp.bfloat16)

    half = chunks // 2
    for at in range(chunks):
        begin = column_of(orders[at])
        cols = pl.ds(begin, chunk)
        value = jnp.zeros((2 * ROWS, chunk), jnp.float32)
        for piece, held_ref in enumerate(held_refs):
            value = value + jnp.dot(
                row_loads[:, piece * PIECE : (piece + 1) * PIECE],
                held_ref[:, cols],
                preferred_element_type=jnp.float32,
            )
        fetch(at).wait()
        value = value + jnp.dot(
            row_loads[:, held:], ring[at % slots], preferred_element_type=jnp.float32
        )
        if at + slots < chunks:
            fetch(at + slots).start()
        place = slice((at % half) * chunk, (at % half + 1) * chunk)
        if at < half:
            send_ref[:, place] = value[:ROWS]
        else:
            keep_ref[:, place] = value[:ROWS]


def product_stage(orders, offsets, place, loads, held, inverse):
    columns = inverse.shape[1]
    chunk = columns // len(orders)
    streamed = inverse.shape[0] - len(held) * PIECE
    slots = SLOTS
    half = jax.ShapeDtypeStruct((ROWS, columns // 2), jnp.float32)
    return pl.pallas_call(
        functools.partial(product_kernel, orders, offsets),
        out_shape=[half, half],
        in_specs=[smem()] + [vmem()] * (len(loads) + len(held)) + [anywhere()],
        out_specs=[vmem(), vmem()],
        scratch_shapes=[
            pltpu.VMEM((slots, streamed, chunk), inverse.dtype),
            pltpu.VMEM((2 * ROWS, inverse.shape[0]), jnp.bfloat16),
            pltpu.SemaphoreType.DMA((slots,)),
        ],
        compiler_params=pltpu.CompilerParams(vmem_limit_bytes=9 * MIB),
        cost_estimate=pl.CostEstimate(
            flops=16 * inverse.shape[0] * columns,
            bytes_accessed=streamed * columns * 2,
            transcendentals=0,
        ),
        name="product",
    )(
        place,
        *loads,
        *[pltpu.with_memory_space_constraint(piece, pltpu.VMEM) for piece in held],
        inverse,
    )


def local(wide, narrow, sensitivity, vol_coord, ctl_coord, pair_list, pair_count, inverse):
    devices = wide * narrow
    components = sensitivity.shape[0]
    ctiles = ctl_coord.shape[1] // CT
    row_count, columns = inverse.shape
    tpb = row_count // CT
    offsets = [
        max((w * narrow + n) * ctiles // devices - w * tpb for w in range(wide))
        for n in range(narrow)
    ]
    tiles = max(offsets) + BAND
    w = lax.axis_index("wide")
    n = lax.axis_index("narrow")
    me = w * narrow + n
    far_tile = (me + devices // 2) % devices * ctiles // devices
    place = jnp.stack([w * tpb, far_tile, w, n]).astype(jnp.int32)
    geometry = (ctiles, tpb, tiles)

    chunk = columns // wide
    fast = (
        narrow == 2
        and wide % 2 == 0
        and chunk % CT == 0
        and tiles <= 2 * tpb
        and max(offsets[0] + BAND, 0) <= tpb
        and row_count == 2048
    )
    if not fast:
        own, spill, far_tile_loads = pair_stage(
            geometry, 0, pair_list, pair_count, place, sensitivity, vol_coord, ctl_coord, inverse
        )
        spans = -(-tiles // tpb)
        band = jnp.pad(spill, ((0, spans * tpb - tiles), (0, 0), (0, 0)))
        block = own
        for shift in range(1, spans):
            part = band[(shift - 1) * tpb : shift * tpb]
            block = block + lax.ppermute(
                part, "wide", [(at, (at + shift) % wide) for at in range(wide)]
            )
        far_row = far_tile % tpb
        far = jnp.zeros((tpb, ROWS, CT), jnp.float32)
        far = lax.dynamic_update_slice(far, far_tile_loads, (far_row, 0, 0))
        far_shift = wide // 2
        block = block + lax.ppermute(
            far, "wide", [(at, (at + far_shift) % wide) for at in range(wide)]
        )
        block = lax.psum(block, "narrow")
        row_loads = block.transpose(1, 0, 2).reshape(ROWS, row_count)[:components]
        terms = jnp.dot(
            row_loads.astype(jnp.bfloat16), inverse, preferred_element_type=jnp.float32
        )
        return lax.psum_scatter(terms, "wide", scatter_dimension=1, tiled=True)

    own, spill, far, *held = pair_stage(
        geometry, HELD, pair_list, pair_count, place, sensitivity, vol_coord, ctl_coord, inverse
    )
    both = ("wide", "narrow")
    partner = lax.ppermute(own, "narrow", [(0, 1), (1, 0)])

    def index(at_w, at_n):
        return (at_w % wide) * narrow + at_n

    spans = range(wide)
    spill_a = lax.ppermute(spill, both, [(index(at, 1), index(at + 1, 0)) for at in spans])
    spill_b = lax.ppermute(spill, both, [(index(at, 1), index(at + 1, 1)) for at in spans])
    half = wide // 2
    far_same = lax.ppermute(far, "wide", [(at, (at + half) % wide) for at in spans])
    far_cross = lax.ppermute(
        far, both, [(index(at, k), index(at + half, 1 - k)) for at in spans for k in range(2)]
    )
    held += hold_stage(HELD, MORE, far, inverse)

    bits = [bit for bit in range(wide.bit_length() - 1)]
    ranks = [
        sum(((at >> (len(bits) - 1 - bit)) & 1) << bit for bit in bits) for at in range(wide)
    ]
    orders = ranks[wide // 2 :] + ranks[: wide // 2]
    send, total = product_stage(
        orders,
        offsets,
        place,
        [own, partner, spill_a, spill_b, far_same, far_cross],
        held,
        inverse,
    )
    for bit in bits:
        moved = lax.ppermute(send, "wide", [(at, at ^ (1 << bit)) for at in spans])
        total = total + moved
        if bit < len(bits) - 1:
            size = total.shape[1] // 2
            total, send = total[:, :size], total[:, size:]
    return total[:components]


def solution(mesh):
    return jax.shard_map(
        functools.partial(local, mesh.shape["wide"], mesh.shape["narrow"]),
        mesh=mesh,
        in_specs=(
            P(None, ("wide", "narrow")),
            P(None, ("wide", "narrow")),
            P(),
            P(None, ("wide", "narrow")),
            P(("wide", "narrow")),
            P("wide", "narrow"),
        ),
        out_specs=P(None, ("narrow", "wide")),
        check_vma=False,
    )
```

time: 295 us -> 94.3 us (0.32)
  blocking collectives: 163 us -> 0 us
  starting transfers between devices: 0.01 us -> 52.7 us
  waiting for transfers between devices: 55.2 us -> 11.8 us
  matrix products: 42.6 us -> 0 us
  Pallas kernels: 0 us -> 25.2 us
  between operations: 14.1 us -> 0.76 us
  local copies, waits for them, and re-layouts: 11.5 us -> 3.61 us
  other arithmetic: 7.44 us -> 0.76 us
    psum x1 -> x0, blocking collectives: 163 us -> none  [local(): whole = lax.psum(loads, ('wide', 'narrow'))]
    reduce_scatter x1 -> x0, waiting for transfers between devices: 55.1 us -> none  [local(): return lax.psum_scatter(col_terms, 'wide', scatter_dimension=1, tiled=True)]
    ppermute x0 -> x9, starting transfers between devices: none -> 52.7 us  [the longest x4 37.3 us: local(): moved = lax.ppermute(send, 'wide', [(at, at ^ 1 << bit) for at in spans])]
    dot_general x3 -> x0, matrix products: 42.6 us -> none  [the longest x1 23.4 us: local(): col_terms = jnp.dot(row_loads, inverse, preferred_element_type=jnp.float32)]
    pallas_call x0 -> x3, Pallas kernels: none -> 25.2 us  [the longest x1 11.2 us: pair_stage(): pl.pallas_call(functools.partial(pair_kernel, geometry, held_count), out_...]
    ppermute x0 -> x9, waiting for transfers between devices: none -> 11.8 us  [the longest x4 11 us: local(): moved = lax.ppermute(send, 'wide', [(at, at ^ 1 << bit) for at in spans])]
    gather x6 -> x0, local copies, waits for them, and re-layouts: 9.6 us -> none  [the longest x2 3.4 us: accumulate(): point_tile = jnp.take(point_tiles, ctl_ids, axis=1)]
    scatter-add x2 -> x0, other arithmetic: 5.56 us -> none  [accumulate(): return acc_sum.at[:, ctl_ids, :].add(terms)]
  transfers between devices with their start and end apart: 1 -> 9, of which waited for: 1 -> 5; matrix products, arithmetic and copies ran while one was open for 0% -> 0% of each run, Pallas kernels for 0% -> 4%
where the time goes in v1:
time: 94.3 us; the launch traced here: 94.8 us
  starting transfers between devices  52.7 us (56%)
  Pallas kernels  25.2 us (27%)
  waiting for transfers between devices  11.8 us (13%)
  local copies, waits for them, and re-layouts  3.61 us (4%)
    ppermute x4, starting transfers between devices, local(): moved = lax.ppermute(send, 'wide', [(at, at ^ 1 << bit) for at in spans])  37.3 us
    pallas_call x1, Pallas kernels, pair_stage(): pl.pallas_call(functools.partial(pair_kernel, geometry, held_count), out_...  11.2 us
    ppermute x4, waiting for transfers between devices, local(): moved = lax.ppermute(send, 'wide', [(at, at ^ 1 << bit) for at in spans])  11 us
    pallas_call x1, Pallas kernels, product_stage(): pl.pallas_call(functools.partial(product_kernel, orders, offsets), out_sh...  10.6 us
    ppermute x1, starting transfers between devices, local(): lax.ppermute(far, both, [(index(at, k), index(at + half, 1 - k)) for at i...  9.68 us
    unnamed x8, local copies, waits for them, and re-layouts  3.58 us
    ppermute x1, starting transfers between devices, local(): partner = lax.ppermute(own, 'narrow', [(0, 1), (1, 0)])  3.43 us
    pallas_call x1, Pallas kernels, hold_stage(): pl.pallas_call(functools.partial(hold_kernel, first), out_shape=[pltpu.VM...  3.39 us
  transfers between devices with their start and end apart: 9, of which 5 were waited for; matrix products, arithmetic and copies ran while one was open for 0% of the time, Pallas kernels for 4%

profile of v1, /device:TPU:0, one launch (start us, length us, event | category | flops | bytes accessed | tf_op | source)
XLA Modules:
  0.0 94.8 jit_solution(14240490774861935175)
XLA Ops:
  0.7 0.1 pad_add_fusion.place_ref
  0.7 0.0 copy-start
  0.7 1.0 %copy-done = f32[3,32768]{1,0:T(4,128)S(1)} copy-done((f32[3,32768]{1,0:T(4,128)S(1)}, f32[3,32768]{1,0:T(4,128)}, u32[]{:S(2)}) %copy-start) | copy-done | bytes 393240
  1.8 0.0 copy-start.1
  1.8 0.9 copy-done.1
  2.7 0.0 copy-start.2
  2.7 0.9 copy-done.2
  3.6 0.0 copy-start.3
  3.6 0.7 copy-done.3
  4.3 11.2 %pairs.1 = (f32[16,8,128]{2,1,0:T(8,128)S(1)}, f32[8,8,128]{2,1,0:T(8,128)S(1)}, f32[1,8,128]{2,1,0:T(8,128)S(1)}, bf16[256,16384]{1,0:T(8,128)(2,1)S(1)}, bf16[...) custom-call(s32[2,512]{1,0:T(2,128)S(1)} %copy-done.3, ...), custom_call_target="tpu_custom_call" | custom-call | flops 3355443200 | bytes 33554432 | tf_op jit(solution)/shard_map/pairs/pallas_call | solution.py:189
  15.5 3.4 %collective-permute-start = (f32[16,8,128]{2,1,0:T(8,128)S(1)}, f32[16,8,128]{2,1,0:T(8,128)S(1)}, u32[]{:S(2)}, u32[]{:S(2)}) collective-permute-start(f32[16,8,128]{2,1,0:T(8,128)S(1)} %get-tuple-element.14.own_ref), channel_id=1, source_target_pairs={{0,1},{1,0},{2,3},{3,2},{4,5},{5,4},{6,7},{7,6},{8,9},{9,8},{10,11... | collective-permute-start | bytes 196616 | tf_op jit(solution)/shard_map/ppermute | solution.py:389
  18.9 0.7 collective-permute-start.2
  19.6 1.3 %collective-permute-start.1 = (f32[8,8,128]{2,1,0:T(8,128)S(1)}, f32[8,8,128]{2,1,0:T(8,128)S(1)}, u32[]{:S(2)}, u32[]{:S(2)}) collective-permute-start(f32[8,8,128]{2,1,0:T(8,128)S(1)} %get-tuple-element.15), channel_id=1, source_target_pairs={{1,2},{3,4},{5,6},{7,8},{9,10},{11,12},{13,14},{15,16},{17,18},{19... | collective-permute-start | bytes 98312 | tf_op jit(solution)/shard_map/ppermute | solution.py:395
  20.9 9.7 %collective-permute-start.4 = (f32[1,8,128]{2,1,0:T(8,128)S(1)}, f32[1,8,128]{2,1,0:T(8,128)S(1)}, u32[]{:S(2)}, u32[]{:S(2)}) collective-permute-start(f32[1,8,128]{2,1,0:T(8,128)S(1)} %get-tuple-element.16.token_ref), channel_id=1, source_target_pairs={{0,17},{1,16},{2,19},{3,18},{4,21},{5,20},{6,23},{7,22},{8,25},{9,... | collective-permute-start | bytes 12296 | tf_op jit(solution)/shard_map/ppermute | solution.py:399
  30.6 0.4 collective-permute-start.3
  30.9 3.4 %hold.1.rest_4_ = bf16[256,16384]{1,0:T(8,128)(2,1)S(1)} custom-call(f32[1,8,128]{2,1,0:T(8,128)S(1)} %get-tuple-element.16.token_ref, bf16[2048,16384]{1,0:T(8,128)(2,1)} %rest_5_.1), custom_call_target="tpu_custom_call" | custom-call | bytes 16777216 | tf_op jit(solution)/shard_map/hold/pallas_call | solution.py:214
  34.3 0.0 collective-permute-done.4.far_cross_ref
  34.4 0.7 collective-permute-done.3.far_same_ref
  35.1 0.0 collective-permute-done.2.spill_b_ref
  35.1 0.0 collective-permute-done.1.spill_a_ref
  35.1 0.0 collective-permute-done.partner_ref
  35.1 10.6 %product.1 = (f32[8,8192]{1,0:T(8,128)S(1)}, f32[8,8192]{1,0:T(8,128)S(1)}) custom-call(s32[4]{0:T(128)S(1)} %pad_add_fusion.place_ref, f32[16,8,128]{2,1,0:T(8,128)S(1)} %get-tuple-element.14.own_ref, f32[16,8,128]{2,1,0:T(8,128)S(1)} %collective-permute-done.partner_ref, f32[8,8,128]{2,1,0:T(8,128)S(1)} %collective-permute-done.1.spill_a_ref, ...), custom_call_target="tpu_custom_call" | custom-call | flops 536870912 | bytes 25165824 | tf_op jit(solution)/shard_map/product/pallas_call | solution.py:307
  45.7 0.1 collective-permute-start.5
  45.8 1.5 %collective-permute-done.5 = f32[8,8192]{1,0:T(8,128)S(1)} collective-permute-done((f32[8,8192]{1,0:T(8,128)S(1)}, f32[8,8192]{1,0:T(8,128)S(1)}, u32[]{:S(2)}, u32[]{:S(2)}) %collective-permute-start.5) | collective-permute-done | bytes 262176 | tf_op jit(solution)/shard_map/ppermute | solution.py:418
  47.4 33.5 %collective-permute-start.6 = (f32[8,4096]{1,0:T(8,128)S(1)}, f32[8,4096]{1,0:T(8,128)S(1)}, u32[]{:S(2)}, u32[]{:S(2)}) collective-permute-start(f32[8,4096]{1,0:T(8,128)S(1)} %slice.29), channel_id=1, source_target_pairs={{0,4},{2,6},{4,0},{6,2},{8,12},{10,14},{12,8},{14,10},{16,20},{18,... | collective-permute-start | bytes 393224 | tf_op jit(solution)/shard_map/ppermute | solution.py:418
  80.9 4.0 %collective-permute-done.6 = f32[8,4096]{1,0:T(8,128)S(1)} collective-permute-done((f32[8,4096]{1,0:T(8,128)S(1)}, f32[8,4096]{1,0:T(8,128)S(1)}, u32[]{:S(2)}, u32[]{:S(2)}) %collective-permute-start.6) | collective-permute-done | bytes 131104 | tf_op jit(solution)/shard_map/ppermute | solution.py:418
  84.9 0.9 collective-permute-start.7
  85.9 3.4 %collective-permute-done.7 = f32[8,2048]{1,0:T(8,128)S(1)} collective-permute-done((f32[8,2048]{1,0:T(8,128)S(1)}, f32[8,2048]{1,0:T(8,128)S(1)}, u32[]{:S(2)}, u32[]{:S(2)}) %collective-permute-start.7) | collective-permute-done | bytes 65568 | tf_op jit(solution)/shard_map/ppermute | solution.py:418
  89.3 2.8 %collective-permute-start.8 = (f32[8,1024]{1,0:T(8,128)S(1)}, f32[8,1024]{1,0:T(8,128)S(1)}, u32[]{:S(2)}, u32[]{:S(2)}) collective-permute-start(f32[8,1024]{1,0:T(8,128)S(1)} %get-tuple-element.24), channel_id=1, source_target_pairs={{0,16},{2,18},{4,20},{6,22},{8,24},{10,26},{12,28},{14,30},{16,0},... | collective-permute-start | bytes 98312 | tf_op jit(solution)/shard_map/ppermute | solution.py:418
  92.1 2.1 %collective-permute-done.8 = f32[8,1024]{1,0:T(8,128)S(1)} collective-permute-done((f32[8,1024]{1,0:T(8,128)S(1)}, f32[8,1024]{1,0:T(8,128)S(1)}, u32[]{:S(2)}, u32[]{:S(2)}) %collective-permute-start.8) | collective-permute-done | bytes 32800 | tf_op jit(solution)/shard_map/ppermute | solution.py:418
  94.2 0.6 slice_add_fusion.2
  (6 shorter events, 0.1 us)
Async XLA Ops:
  0.7 1.0 %copy-start = (f32[3,32768]{1,0:T(4,128)S(1)}, f32[3,32768]{1,0:T(4,128)}, u32[]{:S(2)}) copy-start(f32[3,32768]{1,0:T(4,128)} %ctl_ref.1) | copy-start | bytes 1179652
  1.8 0.9 %copy-start.1 = (f32[6,8192]{1,0:T(8,128)S(1)}, f32[6,8192]{1,0:T(8,128)}, u32[]{:S(2)}) copy-start(f32[6,8192]{1,0:T(8,128)} %sens_ref.1) | copy-start | bytes 589828
  2.7 0.9 copy-start.2
  3.6 0.7 copy-start.3
  15.5 19.6 %collective-permute-start = (f32[16,8,128]{2,1,0:T(8,128)S(1)}, f32[16,8,128]{2,1,0:T(8,128)S(1)}, u32[]{:S(2)}, u32[]{:S(2)}) collective-permute-start(f32[16,8,128]{2,1,0:T(8,128)S(1)} %get-tuple-element.14.own_ref), channel_id=1, source_target_pairs={{0,1},{1,0},{2,3},{3,2},{4,5},{5,4},{6,7},{7,6},{8,9},{9,8},{10,11... | collective-permute-start | bytes 196616 | tf_op jit(solution)/shard_map/ppermute | solution.py:389
  18.9 16.1 %collective-permute-start.2 = (f32[8,8,128]{2,1,0:T(8,128)S(1)}, f32[8,8,128]{2,1,0:T(8,128)S(1)}, u32[]{:S(2)}, u32[]{:S(2)}) collective-permute-start(f32[8,8,128]{2,1,0:T(8,128)S(1)} %get-tuple-element.15), channel_id=1, source_target_pairs={{1,3},{3,5},{5,7},{7,9},{9,11},{11,13},{13,15},{15,17},{17,19},{19... | collective-permute-start | bytes 98312 | tf_op jit(solution)/shard_map/ppermute | solution.py:396
  19.6 15.5 %collective-permute-start.1 = (f32[8,8,128]{2,1,0:T(8,128)S(1)}, f32[8,8,128]{2,1,0:T(8,128)S(1)}, u32[]{:S(2)}, u32[]{:S(2)}) collective-permute-start(f32[8,8,128]{2,1,0:T(8,128)S(1)} %get-tuple-element.15), channel_id=1, source_target_pairs={{1,2},{3,4},{5,6},{7,8},{9,10},{11,12},{13,14},{15,16},{17,18},{19... | collective-permute-start | bytes 98312 | tf_op jit(solution)/shard_map/ppermute | solution.py:395
  20.9 13.4 %collective-permute-start.4 = (f32[1,8,128]{2,1,0:T(8,128)S(1)}, f32[1,8,128]{2,1,0:T(8,128)S(1)}, u32[]{:S(2)}, u32[]{:S(2)}) collective-permute-start(f32[1,8,128]{2,1,0:T(8,128)S(1)} %get-tuple-element.16.token_ref), channel_id=1, source_target_pairs={{0,17},{1,16},{2,19},{3,18},{4,21},{5,20},{6,23},{7,22},{8,25},{9,... | collective-permute-start | bytes 12296 | tf_op jit(solution)/shard_map/ppermute | solution.py:399
  30.6 4.5 %collective-permute-start.3 = (f32[1,8,128]{2,1,0:T(8,128)S(1)}, f32[1,8,128]{2,1,0:T(8,128)S(1)}, u32[]{:S(2)}, u32[]{:S(2)}) collective-permute-start(f32[1,8,128]{2,1,0:T(8,128)S(1)} %get-tuple-element.16.token_ref), channel_id=1, source_target_pairs={{0,16},{2,18},{4,20},{6,22},{8,24},{10,26},{12,28},{14,30},{16,0},... | collective-permute-start | bytes 12296 | tf_op jit(solution)/shard_map/ppermute | solution.py:398
  45.7 1.6 %collective-permute-start.5 = (f32[8,8192]{1,0:T(8,128)S(1)}, f32[8,8192]{1,0:T(8,128)S(1)}, u32[]{:S(2)}, u32[]{:S(2)}) collective-permute-start(f32[8,8192]{1,0:T(8,128)S(1)} %get-tuple-element.22), channel_id=1, source_target_pairs={{0,2},{2,0},{4,6},{6,4},{8,10},{10,8},{12,14},{14,12},{16,18},{18,... | collective-permute-start | bytes 786440 | tf_op jit(solution)/shard_map/ppermute | solution.py:418
  47.4 37.5 %collective-permute-start.6 = (f32[8,4096]{1,0:T(8,128)S(1)}, f32[8,4096]{1,0:T(8,128)S(1)}, u32[]{:S(2)}, u32[]{:S(2)}) collective-permute-start(f32[8,4096]{1,0:T(8,128)S(1)} %slice.29), channel_id=1, source_target_pairs={{0,4},{2,6},{4,0},{6,2},{8,12},{10,14},{12,8},{14,10},{16,20},{18,... | collective-permute-start | bytes 393224 | tf_op jit(solution)/shard_map/ppermute | solution.py:418
  84.9 4.3 %collective-permute-start.7 = (f32[8,2048]{1,0:T(8,128)S(1)}, f32[8,2048]{1,0:T(8,128)S(1)}, u32[]{:S(2)}, u32[]{:S(2)}) collective-permute-start(f32[8,2048]{1,0:T(8,128)S(1)} %slice.31), channel_id=1, source_target_pairs={{0,8},{2,10},{4,12},{6,14},{8,0},{10,2},{12,4},{14,6},{16,24},{18,... | collective-permute-start | bytes 196616 | tf_op jit(solution)/shard_map/ppermute | solution.py:418
  89.3 4.9 %collective-permute-start.8 = (f32[8,1024]{1,0:T(8,128)S(1)}, f32[8,1024]{1,0:T(8,128)S(1)}, u32[]{:S(2)}, u32[]{:S(2)}) collective-permute-start(f32[8,1024]{1,0:T(8,128)S(1)} %get-tuple-element.24), channel_id=1, source_target_pairs={{0,16},{2,18},{4,20},{6,22},{8,24},{10,26},{12,28},{14,30},{16,0},... | collective-permute-start | bytes 98312 | tf_op jit(solution)/shard_map/ppermute | solution.py:418

commit v2 on v1

--- a/solution.py
+++ b/solution.py
@@ -18,6 +18,7 @@
 HELD = 4
 MORE = 1
 SLOTS = 4
+PRODUCT_MIB = 7
 
 
 def thirds(value):
@@ -78,21 +79,37 @@
 ):
     ctiles, tpb, tiles = geometry
     held_refs, rest = rest[:held_count], rest[held_count:]
-    nodes, points, weights, loads_ref = rest[:4]
+    nodes, points, weights, loads_ref, squares, kernels, sens_in, vol_in, ctl_in, in_sems = rest[:10]
     vtiles = vol_ref.shape[1] // VT
-    copies = held_copies(0, inverse_ref, held_refs, rest[4]) if held_count else []
+    slots = list_ref.shape[1]
+    inputs = [
+        pltpu.make_async_copy(source, target, in_sems.at[at])
+        for at, (source, target) in enumerate(
+            [(vol_ref, vol_in), (ctl_ref, ctl_in), (sens_ref, sens_in)]
+        )
+    ]
+    for copy in inputs:
+        copy.start()
+    copies = held_copies(0, inverse_ref, held_refs, rest[10]) if held_count else []
     for copy in copies:
         copy.start()
 
     first_tile = place_ref[0]
     far_tile = place_ref[1]
 
+    loads_ref[...] = jnp.zeros(loads_ref.shape, jnp.float32)
+    squares[...] = jnp.zeros(squares.shape, jnp.float32)
+    kernels[...] = jnp.zeros(kernels.shape, jnp.bfloat16)
+    weights[vtiles] = jnp.zeros(weights.shape[1:], jnp.bfloat16)
+    for copy in inputs:
+        copy.wait()
+
     group = 8
 
     def node_group(group_id, carry):
         begin = pl.multiple_of(group_id * (group * VT), group * VT)
-        rows = features(vol_ref[:, pl.ds(begin, group * VT)], True)
-        sens = sens_ref[:, pl.ds(begin, group * VT)]
+        rows = features(vol_in[:, pl.ds(begin, group * VT)], True)
+        sens = sens_in[:, pl.ds(begin, group * VT)]
         components = sens.shape[0]
         if components < ROWS:
             sens = jnp.concatenate(
@@ -107,48 +124,50 @@
         return carry
 
     lax.fori_loop(0, vtiles // group, node_group, 0)
-    weights[vtiles] = jnp.zeros(weights.shape[1:], jnp.bfloat16)
-
-    def point_tile(tile, carry):
-        named = lax.rem(first_tile + tile, ctiles)
-        named = jnp.where(tile == tiles, far_tile, named)
+
+    for tile in range(tiles + 1):
+        named = lax.rem(first_tile + tile, ctiles) if tile < tiles else far_tile
         begin = pl.multiple_of(named * CT, CT)
-        points[tile] = features(ctl_ref[:, pl.ds(begin, CT)], False).astype(jnp.bfloat16)
-        loads_ref[tile] = jnp.zeros((ROWS, CT), jnp.float32)
-        return carry
-
-    lax.fori_loop(0, tiles + 1, point_tile, 0)
+        points[tile] = features(ctl_in[:, pl.ds(begin, CT)], False).astype(jnp.bfloat16)
 
     count = count_ref[0]
+
+    def tiles_of(slot):
+        live = (slot >= 0) & (slot < count)
+        at = jnp.minimum(jnp.maximum(slot, 0), slots - 1)
+        volume = jnp.where(live, list_ref[0, at], 0)
+        control = list_ref[1, at] - first_tile
+        control = jnp.where(control < 0, control + ctiles, control)
+        control = jnp.where(slot == 0, tiles, control)
+        control = jnp.where(live, control, 0)
+        return live, volume, control
 
     def pairs_step(step_id, carry):
         results = []
         for at in range(UNROLL):
-            slot = step_id * UNROLL + at
-            live = slot < count
-            volume = jnp.where(live, list_ref[0, slot], 0)
-            control = list_ref[1, slot] - first_tile
-            control = jnp.where(control < 0, control + ctiles, control)
-            control = jnp.where(slot == 0, tiles, control)
-            control = jnp.where(live, control, 0)
-            squared = jnp.dot(nodes[volume], points[control], preferred_element_type=jnp.float32)
-            squared = jnp.maximum(squared, 1e-12)
+            live, volume, control = tiles_of((step_id - 2) * UNROLL + at)
+            weight = weights[jnp.where(live, volume, vtiles)]
+            terms = jnp.dot(weight, kernels[at], preferred_element_type=jnp.float32)
+            results.append((control, terms[:ROWS] + terms[ROWS:]))
+        for at in range(UNROLL):
+            squared = jnp.maximum(squares[at], 1e-12)
             radius = squared * lax.rsqrt(squared)
             inside = jnp.maximum(4.0 - radius, 0.0)
             inside = inside * inside
             kernel = inside * inside * (radius + 1.0)
             high = kernel.astype(jnp.bfloat16)
-            low = (kernel - high.astype(jnp.float32)).astype(jnp.bfloat16)
-            weight = weights[jnp.where(live, volume, vtiles)]
-            terms = jnp.dot(
-                weight, jnp.concatenate([high, low], axis=0), preferred_element_type=jnp.float32
+            kernels[at, :VT] = high
+            kernels[at, VT:] = (kernel - high.astype(jnp.float32)).astype(jnp.bfloat16)
+        for at in range(UNROLL):
+            _, volume, control = tiles_of(step_id * UNROLL + at)
+            squares[at] = jnp.dot(
+                nodes[volume], points[control], preferred_element_type=jnp.float32
             )
-            results.append((control, terms[:ROWS] + terms[ROWS:]))
         for control, terms in results:
             loads_ref[control] = loads_ref[control] + terms
         return carry
 
-    lax.fori_loop(0, (count + UNROLL - 1) // UNROLL, pairs_step, 0)
+    lax.fori_loop(0, (count + UNROLL - 1) // UNROLL + 2, pairs_step, 0)
     own_ref[...] = loads_ref[:tpb] * (1.0 / 256.0)
     spill_ref[...] = loads_ref[tpb:tiles] * (1.0 / 256.0)
     far_ref[...] = loads_ref[tiles:] * (1.0 / 256.0)
@@ -165,7 +184,7 @@
 
 
 def anywhere():
-    return pl.BlockSpec(memory_space=pl.ANY)
+    return pl.BlockSpec(memory_space=pltpu.HBM)
 
 
 def pair_stage(geometry, held_count, pair_list, pair_count, place, sens, vol, ctl, inverse):
@@ -181,6 +200,12 @@
         pltpu.VMEM((tiles + 1, DEPTH, CT), jnp.bfloat16),
         pltpu.VMEM((vtiles + 1, 2 * ROWS, 2 * VT), jnp.bfloat16),
         pltpu.VMEM((tiles + 1, ROWS, CT), jnp.float32),
+        pltpu.VMEM((UNROLL, VT, CT), jnp.float32),
+        pltpu.VMEM((UNROLL, 2 * VT, CT), jnp.bfloat16),
+        pltpu.VMEM(sens.shape, jnp.float32),
+        pltpu.VMEM(vol.shape, jnp.float32),
+        pltpu.VMEM(ctl.shape, jnp.float32),
+        pltpu.SemaphoreType.DMA((3,)),
     ]
     if held_count:
         out_shape += [pltpu.VMEM((PIECE, columns), inverse.dtype)] * held_count
@@ -189,7 +214,7 @@
     return pl.pallas_call(
         functools.partial(pair_kernel, geometry, held_count),
         out_shape=out_shape,
-        in_specs=[smem(), smem(), smem(), vmem(), vmem(), vmem(), anywhere()],
+        in_specs=[smem(), smem(), smem()] + [anywhere()] * 4,
         out_specs=out_specs,
         scratch_shapes=scratch,
         compiler_params=pltpu.CompilerParams(vmem_limit_bytes=10 * MIB),
@@ -225,7 +250,52 @@
     )(token, inverse)
 
 
-def product_kernel(
+def multiply(orders, me, row_loads, held_refs, inverse_ref, out_refs, partial, ring, sems):
+    streamed = ring.shape[1]
+    held = inverse_ref.shape[0] - streamed
+    chunk = ring.shape[2]
+    slots = ring.shape[0]
+    count = len(orders)
+    per_out = count // len(out_refs)
+
+    def columns_of(at):
+        return pl.ds(pl.multiple_of((me ^ orders[at]) * chunk, chunk), chunk)
+
+    def fetch(at):
+        return pltpu.make_async_copy(
+            inverse_ref.at[pl.ds(held, streamed), columns_of(at)],
+            ring.at[at % slots],
+            sems.at[at % slots],
+        )
+
+    for at in range(slots):
+        fetch(at).start()
+    yield
+    for at in range(count):
+        value = jnp.zeros((2 * ROWS, chunk), jnp.float32)
+        for piece, held_ref in enumerate(held_refs):
+            value = value + jnp.dot(
+                row_loads[:, piece * PIECE : (piece + 1) * PIECE],
+                held_ref[:, columns_of(at)],
+                preferred_element_type=jnp.float32,
+            )
+        partial[at] = value[:ROWS]
+    for at in range(count):
+        fetch(at).wait()
+        value = jnp.dot(
+            row_loads[:, held:], ring[at % slots], preferred_element_type=jnp.float32
+        )
+        if at + slots < count:
+            fetch(at + slots).start()
+        out_ref = out_refs[at // per_out]
+        place = at % per_out
+        out_ref[:, place * chunk : (place + 1) * chunk] = (partial[at] + value[:ROWS]).astype(
+            out_ref.dtype
+        )
+    yield
+
+
+def first_kernel(
     orders,
     offsets,
     place_ref,
@@ -237,32 +307,23 @@
     far_cross_ref,
     *rest,
 ):
-    held_refs = rest[:-6]
-    inverse_ref, send_ref, keep_ref, ring, row_loads, sems = rest[-6:]
+    held_refs = rest[:-8]
+    inverse_ref, row_loads, *out_refs, partial, ring, sems = rest[-8:]
     tpb = partner_ref.shape[0]
     spilled = spill_a_ref.shape[0]
-    chunks = len(orders)
-    columns = inverse_ref.shape[1]
-    chunk = columns // chunks
-    slots = ring.shape[0]
-    streamed = ring.shape[1]
-    held = inverse_ref.shape[0] - streamed
-    me = place_ref[2]
     even = place_ref[3] == 0
-
-    def column_of(order):
-        return pl.multiple_of((me ^ order) * chunk, chunk)
-
-    def fetch(at):
-        return pltpu.make_async_copy(
-            inverse_ref.at[pl.ds(held, streamed), pl.ds(column_of(orders[at]), chunk)],
-            ring.at[at % slots],
-            sems.at[at % slots],
-        )
-
-    for at in range(slots):
-        fetch(at).start()
-
+    steps = multiply(
+        orders,
+        place_ref[2],
+        row_loads,
+        held_refs,
+        inverse_ref,
+        out_refs,
+        partial,
+        ring,
+        sems,
+    )
+    next(steps)
     for tile in range(tpb):
         total = own_ref[tile] + partner_ref[tile]
         if tile < spilled:
@@ -273,57 +334,50 @@
             total = total + jnp.where(even, far_cross_ref[0], far_same_ref[0])
         both = jnp.concatenate([total, jnp.zeros_like(total)], axis=0)
         row_loads[:, tile * CT : (tile + 1) * CT] = both.astype(jnp.bfloat16)
-
-    half = chunks // 2
-    for at in range(chunks):
-        begin = column_of(orders[at])
-        cols = pl.ds(begin, chunk)
-        value = jnp.zeros((2 * ROWS, chunk), jnp.float32)
-        for piece, held_ref in enumerate(held_refs):
-            value = value + jnp.dot(
-                row_loads[:, piece * PIECE : (piece + 1) * PIECE],
-                held_ref[:, cols],
-                preferred_element_type=jnp.float32,
-            )
-        fetch(at).wait()
-        value = value + jnp.dot(
-            row_loads[:, held:], ring[at % slots], preferred_element_type=jnp.float32
-        )
-        if at + slots < chunks:
-            fetch(at + slots).start()
-        place = slice((at % half) * chunk, (at % half + 1) * chunk)
-        if at < half:
-            send_ref[:, place] = value[:ROWS]
-        else:
-            keep_ref[:, place] = value[:ROWS]
-
-
-def product_stage(orders, offsets, place, loads, held, inverse):
-    columns = inverse.shape[1]
-    chunk = columns // len(orders)
-    streamed = inverse.shape[0] - len(held) * PIECE
-    slots = SLOTS
-    half = jax.ShapeDtypeStruct((ROWS, columns // 2), jnp.float32)
+    next(steps)
+
+
+def next_kernel(orders, place_ref, row_loads, *rest):
+    held_refs = rest[:-5]
+    inverse_ref, out_ref, partial, ring, sems = rest[-5:]
+    steps = multiply(
+        orders,
+        place_ref[2],
+        row_loads,
+        held_refs,
+        inverse_ref,
+        [out_ref],
+        partial,
+        ring,
+        sems,
+    )
+    next(steps)
+    next(steps)
+
+
+def product_stage(kernel, orders, chunk, small, held, inverse, outs, name):
+    rows = inverse.shape[0]
+    streamed = rows - len(held) * PIECE
+    slots = min(SLOTS, len(orders))
     return pl.pallas_call(
-        functools.partial(product_kernel, orders, offsets),
-        out_shape=[half, half],
-        in_specs=[smem()] + [vmem()] * (len(loads) + len(held)) + [anywhere()],
-        out_specs=[vmem(), vmem()],
+        kernel,
+        out_shape=outs,
+        in_specs=[smem()] + [vmem()] * (len(small) - 1 + len(held)) + [anywhere()],
+        out_specs=[vmem()] * len(outs),
         scratch_shapes=[
+            pltpu.VMEM((len(orders), ROWS, chunk), jnp.float32),
             pltpu.VMEM((slots, streamed, chunk), inverse.dtype),
-            pltpu.VMEM((2 * ROWS, inverse.shape[0]), jnp.bfloat16),
             pltpu.SemaphoreType.DMA((slots,)),
         ],
-        compiler_params=pltpu.CompilerParams(vmem_limit_bytes=9 * MIB),
+        compiler_params=pltpu.CompilerParams(vmem_limit_bytes=PRODUCT_MIB * MIB),
         cost_estimate=pl.CostEstimate(
-            flops=16 * inverse.shape[0] * columns,
-            bytes_accessed=streamed * columns * 2,
+            flops=16 * rows * chunk * len(orders),
+            bytes_accessed=rows * chunk * len(orders),
             transcendentals=0,
         ),
-        name="product",
+        name=name,
     )(
-        place,
-        *loads,
+        *small,
         *[pltpu.with_memory_space_constraint(piece, pltpu.VMEM) for piece in held],
         inverse,
     )
@@ -350,11 +404,12 @@
     chunk = columns // wide
     fast = (
         narrow == 2
-        and wide % 2 == 0
+        and wide >= 8
+        and wide & (wide - 1) == 0
         and chunk % CT == 0
         and tiles <= 2 * tpb
         and max(offsets[0] + BAND, 0) <= tpb
-        and row_count == 2048
+        and row_count == 8 * PIECE
     )
     if not fast:
         own, spill, far_tile_loads = pair_stage(
@@ -392,35 +447,64 @@
         return (at_w % wide) * narrow + at_n
 
     spans = range(wide)
-    spill_a = lax.ppermute(spill, both, [(index(at, 1), index(at + 1, 0)) for at in spans])
-    spill_b = lax.ppermute(spill, both, [(index(at, 1), index(at + 1, 1)) for at in spans])
     half = wide // 2
-    far_same = lax.ppermute(far, "wide", [(at, (at + half) % wide) for at in spans])
-    far_cross = lax.ppermute(
-        far, both, [(index(at, k), index(at + half, 1 - k)) for at in spans for k in range(2)]
-    )
+    straight = [lambda at, k=k: (at, (at + k) % wide) for k in (1, half)]
+    cross = [
+        [(index(at, k), index(at + shift, 1 - k)) for at in spans for k in range(2)]
+        for shift in (1, half)
+    ]
+    spill_b = lax.ppermute(spill, "wide", [straight[0](at) for at in spans])
+    spill_a = lax.ppermute(spill, both, cross[0])
+    far_same = lax.ppermute(far, "wide", [straight[1](at) for at in spans])
+    far_cross = lax.ppermute(far, both, cross[1])
     held += hold_stage(HELD, MORE, far, inverse)
 
-    bits = [bit for bit in range(wide.bit_length() - 1)]
-    ranks = [
-        sum(((at >> (len(bits) - 1 - bit)) & 1) << bit for bit in bits) for at in range(wide)
-    ]
-    orders = ranks[wide // 2 :] + ranks[: wide // 2]
-    send, total = product_stage(
+    ends = range(wide // 4)
+    quarter = columns // 4
+
+    def orders_of(near):
+        return [near | (end << 2) for end in ends]
+
+    orders = orders_of(3) + orders_of(2) + orders_of(1)
+    row_loads, part_3, part_2, part_1 = product_stage(
+        functools.partial(first_kernel, orders, offsets),
         orders,
-        offsets,
-        place,
-        [own, partner, spill_a, spill_b, far_same, far_cross],
+        chunk,
+        [place, own, partner, spill_a, spill_b, far_same, far_cross],
         held,
         inverse,
-    )
-    for bit in bits:
-        moved = lax.ppermute(send, "wide", [(at, at ^ (1 << bit)) for at in spans])
-        total = total + moved
-        if bit < len(bits) - 1:
-            size = total.shape[1] // 2
-            total, send = total[:, :size], total[:, size:]
-    return total[:components]
+        [
+            pltpu.VMEM((2 * ROWS, row_count), jnp.bfloat16),
+            jax.ShapeDtypeStruct((ROWS, quarter), jnp.bfloat16),
+            jax.ShapeDtypeStruct((ROWS, quarter), jnp.bfloat16),
+            jax.ShapeDtypeStruct((ROWS, quarter), jnp.float32),
+        ],
+        "product_a",
+    )
+
+    def to(difference, value):
+        return lax.ppermute(value, "wide", [(at, at ^ difference) for at in spans])
+
+    part_3 = to(3, part_3)
+    part_2 = to(2, part_2)
+    part_1 = to(1, part_1)
+    orders = orders_of(0)
+    (part_0,) = product_stage(
+        functools.partial(next_kernel, orders),
+        orders,
+        chunk,
+        [place, row_loads],
+        held,
+        inverse,
+        [jax.ShapeDtypeStruct((ROWS, quarter), jnp.float32)],
+        "product_b",
+    )
+    total = part_0 + part_1 + part_3.astype(jnp.float32) + part_2.astype(jnp.float32)
+    result = total[:, :chunk]
+    for end in ends[1:]:
+        sent = total[:, end * chunk : (end + 1) * chunk].astype(jnp.bfloat16)
+        result = result + to(end << 2, sent).astype(jnp.float32)
+    return result[:components]
 
 
 def solution(mesh):

time: 94.3 us -> 74.4 us (0.79)
  starting transfers between devices: 52.7 us -> 33.5 us
  waiting for transfers between devices: 11.8 us -> 5.24 us
  Pallas kernels: 25.2 us -> 31.4 us
    ppermute x8 -> x10, starting transfers between devices: 49.3 us -> 30.5 us  [the longest x6 24.9 us: to(): return lax.ppermute(value, 'wide', [(at, at ^ difference) for at in spans])]
    ppermute x8 -> x10, waiting for transfers between devices: 11.8 us -> 5.24 us  [the longest x6 4.47 us: to(): return lax.ppermute(value, 'wide', [(at, at ^ difference) for at in spans])]
    pallas_call x1 -> x2, Pallas kernels: 10.6 us -> 16.6 us  [product_stage(): pl.pallas_call(kernel, out_shape=outs, in_specs=[smem()] + [vmem()] * (le...]
  transfers between devices with their start and end apart: 9 -> 11, of which waited for: 5 -> 4; matrix products, arithmetic and copies ran while one was open for 0% -> 0% of each run, Pallas kernels for 4% -> 11%
where the time goes in v2:
time: 74.4 us; the launch traced here: 75.3 us
  starting transfers between devices  33.5 us (45%)
  Pallas kernels  31.4 us (42%)
  waiting for transfers between devices  5.24 us (7%)
  local copies, waits for them, and re-layouts  3.59 us (5%)
  between operations  0.77 us (1%)
    ppermute x6, starting transfers between devices, to(): return lax.ppermute(value, 'wide', [(at, at ^ difference) for at in spans])  24.9 us
    pallas_call x2, Pallas kernels, product_stage(): pl.pallas_call(kernel, out_shape=outs, in_specs=[smem()] + [vmem()] * (le...  16.6 us
    pallas_call x1, Pallas kernels, pair_stage(): pl.pallas_call(functools.partial(pair_kernel, geometry, held_count), out_...  11.4 us
    ppermute x6, waiting for transfers between devices, to(): return lax.ppermute(value, 'wide', [(at, at ^ difference) for at in spans])  4.47 us
    unnamed x8, local copies, waits for them, and re-layouts  3.58 us
    ppermute x1, starting transfers between devices, local(): far_cross = lax.ppermute(far, both, cross[1])  3.54 us
    pallas_call x1, Pallas kernels, hold_stage(): pl.pallas_call(functools.partial(hold_kernel, first), out_shape=[pltpu.VM...  3.39 us
    ppermute x1, starting transfers between devices, local(): partner = lax.ppermute(own, 'narrow', [(0, 1), (1, 0)])  3.03 us
  transfers between devices with their start and end apart: 11, of which 4 were waited for; matrix products, arithmetic and copies ran while one was open for 0% of the time, Pallas kernels for 11%

profile of v2, /device:TPU:0, one launch (start us, length us, event | category | flops | bytes accessed | tf_op | source)
XLA Modules:
  0.0 75.3 jit_solution(13506901306870288078)
XLA Ops:
  0.7 0.1 pad_add_fusion.place_ref
  0.7 1.0 %copy-done = f32[3,32768]{1,0:T(4,128)S(1)} copy-done((f32[3,32768]{1,0:T(4,128)S(1)}, f32[3,32768]{1,0:T(4,128)}, u32[]{:S(2)}) %copy-start) | copy-done | bytes 393240
  1.8 0.9 %copy-done.1 = f32[6,8192]{1,0:T(8,128)S(1)} copy-done((f32[6,8192]{1,0:T(8,128)S(1)}, f32[6,8192]{1,0:T(8,128)}, u32[]{:S(2)}) %copy-start.1) | copy-done | bytes 196632
  2.7 0.9 %copy-done.2 = f32[3,8192]{1,0:T(4,128)S(1)} copy-done((f32[3,8192]{1,0:T(4,128)S(1)}, f32[3,8192]{1,0:T(4,128)}, u32[]{:S(2)}) %copy-start.2) | copy-done | bytes 98328
  3.6 0.7 copy-done.3
  4.3 11.4 %pairs.1 = (f32[16,8,128]{2,1,0:T(8,128)S(1)}, f32[8,8,128]{2,1,0:T(8,128)S(1)}, f32[1,8,128]{2,1,0:T(8,128)S(1)}, bf16[256,16384]{1,0:T(8,128)(2,1)S(1)}, bf16[...) custom-call(s32[2,512]{1,0:T(2,128)S(1)} %copy-done.3, ...), custom_call_target="tpu_custom_call" | custom-call | flops 3355443200 | bytes 33554432 | tf_op jit(solution)/shard_map/pairs/pallas_call | solution.py:214
  15.8 3.0 %collective-permute-start = (f32[16,8,128]{2,1,0:T(8,128)S(1)}, f32[16,8,128]{2,1,0:T(8,128)S(1)}, u32[]{:S(2)}, u32[]{:S(2)}) collective-permute-start(f32[16,8,128]{2,1,0:T(8,128)S(1)} %get-tuple-element.16.own_ref), channel_id=1, source_target_pairs={{0,1},{1,0},{2,3},{3,2},{4,5},{5,4},{6,7},{7,6},{8,9},{9,8},{10,11... | collective-permute-start | bytes 196616 | tf_op jit(solution)/shard_map/ppermute | solution.py:444
  18.8 0.0 collective-permute-start.2
  18.8 1.7 %collective-permute-start.1 = (f32[8,8,128]{2,1,0:T(8,128)S(1)}, f32[8,8,128]{2,1,0:T(8,128)S(1)}, u32[]{:S(2)}, u32[]{:S(2)}) collective-permute-start(f32[8,8,128]{2,1,0:T(8,128)S(1)} %get-tuple-element.17), channel_id=1, source_target_pairs={{0,3},{1,2},{2,5},{3,4},{4,7},{5,6},{6,9},{7,8},{8,11},{9,10},{10,... | collective-permute-start | bytes 98312 | tf_op jit(solution)/shard_map/ppermute | solution.py:457
  20.5 3.5 %collective-permute-start.4 = (f32[1,8,128]{2,1,0:T(8,128)S(1)}, f32[1,8,128]{2,1,0:T(8,128)S(1)}, u32[]{:S(2)}, u32[]{:S(2)}) collective-permute-start(f32[1,8,128]{2,1,0:T(8,128)S(1)} %get-tuple-element.18.token_ref), channel_id=1, source_target_pairs={{0,17},{1,16},{2,19},{3,18},{4,21},{5,20},{6,23},{7,22},{8,25},{9,... | collective-permute-start | bytes 12296 | tf_op jit(solution)/shard_map/ppermute | solution.py:459
  24.1 0.3 collective-permute-start.3
  24.4 3.4 %hold.1.rest_4_ = bf16[256,16384]{1,0:T(8,128)(2,1)S(1)} custom-call(f32[1,8,128]{2,1,0:T(8,128)S(1)} %get-tuple-element.18.token_ref, bf16[2048,16384]{1,0:T(8,128)(2,1)} %rest_5_.3), custom_call_target="tpu_custom_call" | custom-call | bytes 16777216 | tf_op jit(solution)/shard_map/hold/pallas_call | solution.py:239
  27.8 0.0 collective-permute-done.4.far_cross_ref
  27.8 0.8 %collective-permute-done.3.far_same_ref = f32[1,8,128]{2,1,0:T(8,128)S(1)} collective-permute-done((f32[1,8,128]{2,1,0:T(8,128)S(1)}, f32[1,8,128]{2,1,0:T(8,128)S(1)}, u32[]{:S(2)}, u32[]{:S(2)}) %collective-permute-start.3) | collective-permute-done | bytes 4128 | tf_op jit(solution)/shard_map/ppermute | solution.py:458
  28.6 0.0 collective-permute-done.2.spill_b_ref
  28.6 0.0 collective-permute-done.1.spill_a_ref
  28.6 0.0 collective-permute-done.partner_ref
  28.6 11.6 %product_a.1 = (bf16[16,2048]{1,0:T(8,128)(2,1)S(1)}, bf16[8,4096]{1,0:T(8,128)(2,1)S(1)}, bf16[8,4096]{1,0:T(8,128)(2,1)S(1)}, f32[8,4096]{1,0:T(8,128)S(1)}) custom-call(s32[4]{0:T(128)S(1)} %pad_add_fusion.place_ref, f32[16,8,128]{2,1,0:T(8,128)S(1)} %get-tuple-element.16.own_ref, f32[16,8,128]{2,1,0:T(8,128)S(1)} %collective-permute-done.partner_ref, ...), custom_call_target="tpu_custom_call" | custom-call | flops 402653184 | bytes 25165824 | tf_op jit(solution)/shard_map/product_a/pallas_call | solution.py:362
  40.2 0.1 collective-permute-start.5
  40.3 21.2 %collective-permute-start.6 = (bf16[8,4096]{1,0:T(8,128)(2,1)S(1)}, bf16[8,4096]{1,0:T(8,128)(2,1)S(1)}, u32[]{:S(2)}, u32[]{:S(2)}) collective-permute-start(bf16[8,4096]{1,0:T(8,128)(2,1)S(1)} %get-tuple-element.25), channel_id=1, source_target_pairs={{0,6},{2,4},{4,2},{6,0},{8,14},{10,12},{12,10},{14,8},{16,22},{18,... | collective-permute-start | bytes 196616 | tf_op jit(solution)/shard_map/ppermute | solution.py:486
  61.5 0.0 collective-permute-start.7
  61.6 5.0 %product_b.1 = f32[8,4096]{1,0:T(8,128)S(1)} custom-call(s32[4]{0:T(128)S(1)} %pad_add_fusion.place_ref, bf16[16,2048]{1,0:T(8,128)(2,1)S(1)} %get-tuple-element.23.row_loads, bf16[256,16384]{1,0:T(8,128)(2,1)S(1)} %get-tuple-element.19.rest_0_, bf16[256,16384]{1,0:T(8,128)(2,1)S(1)} %get-tuple-element.20.rest_1_, ...), custom_call_target="tpu_custom_call" | custom-call | flops 134217728 | bytes 8388608 | tf_op jit(solution)/shard_map/product_b/pallas_call | solution.py:362
  66.6 0.0 collective-permute-done.6
  66.6 0.0 collective-permute-done.7
  66.6 0.0 collective-permute-done.5
  66.7 0.1 collective-permute-start.8
  66.7 3.3 %collective-permute-start.10 = (bf16[8,1024]{1,0:T(8,128)(2,1)S(1)}, bf16[8,1024]{1,0:T(8,128)(2,1)S(1)}, u32[]{:S(2)}, u32[]{:S(2)}) collective-permute-start(bf16[8,1024]{1,0:T(8,128)(2,1)S(1)} %get-tuple-element.30), channel_id=1, source_target_pairs={{0,24},{2,26},{4,28},{6,30},{8,16},{10,18},{12,20},{14,22},{16,8},... | collective-permute-start | bytes 49160 | tf_op jit(solution)/shard_map/ppermute | solution.py:486
  70.0 0.2 collective-permute-start.9
  70.2 0.2 collective-permute-done.8
  70.5 1.9 %collective-permute-done.10 = bf16[8,1024]{1,0:T(8,128)(2,1)S(1)} collective-permute-done((bf16[8,1024]{1,0:T(8,128)(2,1)S(1)}, bf16[8,1024]{1,0:T(8,128)(2,1)S(1)}, u32[]{:S(2)}, u32[]{:S(2)}) %collective-permute-start.10) | collective-permute-done | bytes 16416 | tf_op jit(solution)/shard_map/ppermute | solution.py:486
  72.3 2.3 %collective-permute-done.9 = bf16[8,1024]{1,0:T(8,128)(2,1)S(1)} collective-permute-done((bf16[8,1024]{1,0:T(8,128)(2,1)S(1)}, bf16[8,1024]{1,0:T(8,128)(2,1)S(1)}, u32[]{:S(2)}, u32[]{:S(2)}) %collective-permute-start.9) | collective-permute-done | bytes 16416 | tf_op jit(solution)/shard_map/ppermute | solution.py:486
  74.7 0.6 fusion.1
  (7 shorter events, 0.1 us)
Async XLA Ops:
  0.7 1.0 %copy-start = (f32[3,32768]{1,0:T(4,128)S(1)}, f32[3,32768]{1,0:T(4,128)}, u32[]{:S(2)}) copy-start(f32[3,32768]{1,0:T(4,128)} %ctl_ref.1) | copy-start | bytes 1179652
  1.8 0.9 %copy-start.1 = (f32[6,8192]{1,0:T(8,128)S(1)}, f32[6,8192]{1,0:T(8,128)}, u32[]{:S(2)}) copy-start(f32[6,8192]{1,0:T(8,128)} %sens_ref.1) | copy-start | bytes 589828
  2.7 0.9 %copy-start.2 = (f32[3,8192]{1,0:T(4,128)S(1)}, f32[3,8192]{1,0:T(4,128)}, u32[]{:S(2)}) copy-start(f32[3,8192]{1,0:T(4,128)} %vol_ref.1) | copy-start | bytes 294916
  3.6 0.7 copy-start.3
  15.8 12.8 %collective-permute-start = (f32[16,8,128]{2,1,0:T(8,128)S(1)}, f32[16,8,128]{2,1,0:T(8,128)S(1)}, u32[]{:S(2)}, u32[]{:S(2)}) collective-permute-start(f32[16,8,128]{2,1,0:T(8,128)S(1)} %get-tuple-element.16.own_ref), channel_id=1, source_target_pairs={{0,1},{1,0},{2,3},{3,2},{4,5},{5,4},{6,7},{7,6},{8,9},{9,8},{10,11... | collective-permute-start | bytes 196616 | tf_op jit(solution)/shard_map/ppermute | solution.py:444
  18.8 9.8 %collective-permute-start.2 = (f32[8,8,128]{2,1,0:T(8,128)S(1)}, f32[8,8,128]{2,1,0:T(8,128)S(1)}, u32[]{:S(2)}, u32[]{:S(2)}) collective-permute-start(f32[8,8,128]{2,1,0:T(8,128)S(1)} %get-tuple-element.17), channel_id=1, source_target_pairs={{0,2},{2,4},{4,6},{6,8},{8,10},{10,12},{12,14},{14,16},{16,18},{18... | collective-permute-start | bytes 98312 | tf_op jit(solution)/shard_map/ppermute | solution.py:456
  18.8 9.8 %collective-permute-start.1 = (f32[8,8,128]{2,1,0:T(8,128)S(1)}, f32[8,8,128]{2,1,0:T(8,128)S(1)}, u32[]{:S(2)}, u32[]{:S(2)}) collective-permute-start(f32[8,8,128]{2,1,0:T(8,128)S(1)} %get-tuple-element.17), channel_id=1, source_target_pairs={{0,3},{1,2},{2,5},{3,4},{4,7},{5,6},{6,9},{7,8},{8,11},{9,10},{10,... | collective-permute-start | bytes 98312 | tf_op jit(solution)/shard_map/ppermute | solution.py:457
  20.5 7.3 %collective-permute-start.4 = (f32[1,8,128]{2,1,0:T(8,128)S(1)}, f32[1,8,128]{2,1,0:T(8,128)S(1)}, u32[]{:S(2)}, u32[]{:S(2)}) collective-permute-start(f32[1,8,128]{2,1,0:T(8,128)S(1)} %get-tuple-element.18.token_ref), channel_id=1, source_target_pairs={{0,17},{1,16},{2,19},{3,18},{4,21},{5,20},{6,23},{7,22},{8,25},{9,... | collective-permute-start | bytes 12296 | tf_op jit(solution)/shard_map/ppermute | solution.py:459
  24.1 4.5 %collective-permute-start.3 = (f32[1,8,128]{2,1,0:T(8,128)S(1)}, f32[1,8,128]{2,1,0:T(8,128)S(1)}, u32[]{:S(2)}, u32[]{:S(2)}) collective-permute-start(f32[1,8,128]{2,1,0:T(8,128)S(1)} %get-tuple-element.18.token_ref), channel_id=1, source_target_pairs={{0,16},{2,18},{4,20},{6,22},{8,24},{10,26},{12,28},{14,30},{16,0},... | collective-permute-start | bytes 12296 | tf_op jit(solution)/shard_map/ppermute | solution.py:458
  40.2 26.4 %collective-permute-start.5 = (f32[8,4096]{1,0:T(8,128)S(1)}, f32[8,4096]{1,0:T(8,128)S(1)}, u32[]{:S(2)}, u32[]{:S(2)}) collective-permute-start(f32[8,4096]{1,0:T(8,128)S(1)} %get-tuple-element.24), channel_id=1, source_target_pairs={{0,2},{2,0},{4,6},{6,4},{8,10},{10,8},{12,14},{14,12},{16,18},{18,... | collective-permute-start | bytes 393224 | tf_op jit(solution)/shard_map/ppermute | solution.py:486
  40.3 26.3 %collective-permute-start.6 = (bf16[8,4096]{1,0:T(8,128)(2,1)S(1)}, bf16[8,4096]{1,0:T(8,128)(2,1)S(1)}, u32[]{:S(2)}, u32[]{:S(2)}) collective-permute-start(bf16[8,4096]{1,0:T(8,128)(2,1)S(1)} %get-tuple-element.25), channel_id=1, source_target_pairs={{0,6},{2,4},{4,2},{6,0},{8,14},{10,12},{12,10},{14,8},{16,22},{18,... | collective-permute-start | bytes 196616 | tf_op jit(solution)/shard_map/ppermute | solution.py:486
  61.5 5.1 %collective-permute-start.7 = (bf16[8,4096]{1,0:T(8,128)(2,1)S(1)}, bf16[8,4096]{1,0:T(8,128)(2,1)S(1)}, u32[]{:S(2)}, u32[]{:S(2)}) collective-permute-start(bf16[8,4096]{1,0:T(8,128)(2,1)S(1)} %get-tuple-element.26), channel_id=1, source_target_pairs={{0,4},{2,6},{4,0},{6,2},{8,12},{10,14},{12,8},{14,10},{16,20},{18,... | collective-permute-start | bytes 196616 | tf_op jit(solution)/shard_map/ppermute | solution.py:486
  66.7 3.8 %collective-permute-start.8 = (bf16[8,1024]{1,0:T(8,128)(2,1)S(1)}, bf16[8,1024]{1,0:T(8,128)(2,1)S(1)}, u32[]{:S(2)}, u32[]{:S(2)}) collective-permute-start(bf16[8,1024]{1,0:T(8,128)(2,1)S(1)} %get-tuple-element.29), channel_id=1, source_target_pairs={{0,8},{2,10},{4,12},{6,14},{8,0},{10,2},{12,4},{14,6},{16,24},{18,... | collective-permute-start | bytes 49160 | tf_op jit(solution)/shard_map/ppermute | solution.py:486
  66.7 5.6 %collective-permute-start.10 = (bf16[8,1024]{1,0:T(8,128)(2,1)S(1)}, bf16[8,1024]{1,0:T(8,128)(2,1)S(1)}, u32[]{:S(2)}, u32[]{:S(2)}) collective-permute-start(bf16[8,1024]{1,0:T(8,128)(2,1)S(1)} %get-tuple-element.30), channel_id=1, source_target_pairs={{0,24},{2,26},{4,28},{6,30},{8,16},{10,18},{12,20},{14,22},{16,8},... | collective-permute-start | bytes 49160 | tf_op jit(solution)/shard_map/ppermute | solution.py:486
  70.0 4.6 %collective-permute-start.9 = (bf16[8,1024]{1,0:T(8,128)(2,1)S(1)}, bf16[8,1024]{1,0:T(8,128)(2,1)S(1)}, u32[]{:S(2)}, u32[]{:S(2)}) collective-permute-start(bf16[8,1024]{1,0:T(8,128)(2,1)S(1)} %get-tuple-element.31), channel_id=1, source_target_pairs={{0,16},{2,18},{4,20},{6,22},{8,24},{10,26},{12,28},{14,30},{16,0},... | collective-permute-start | bytes 49160 | tf_op jit(solution)/shard_map/ppermute | solution.py:486

commit v3 on v2

--- a/solution.py
+++ b/solution.py
@@ -10,13 +10,14 @@
 CT = 128
 VT = 128
 BAND = 16
-UNROLL = 4
+UNROLL = 8
+AHEAD = 2
 ROWS = 8
 DEPTH = 64
 MIB = 1 << 20
 PIECE = 256
-HELD = 4
-MORE = 1
+HELD = 5
+MORE = 0
 SLOTS = 4
 PRODUCT_MIB = 7
 
@@ -65,9 +66,9 @@
 def pair_kernel(
     geometry,
     held_count,
-    list_ref,
     count_ref,
     place_ref,
+    listed_ref,
     sens_ref,
     vol_ref,
     ctl_ref,
@@ -79,18 +80,25 @@
 ):
     ctiles, tpb, tiles = geometry
     held_refs, rest = rest[:held_count], rest[held_count:]
-    nodes, points, weights, loads_ref, squares, kernels, sens_in, vol_in, ctl_in, in_sems = rest[:10]
+    nodes, points, weights, loads_ref, squares, kernels, sens_in, vol_in, ctl_in, list_ref, in_sems = (
+        rest[:11]
+    )
     vtiles = vol_ref.shape[1] // VT
     slots = list_ref.shape[1]
     inputs = [
         pltpu.make_async_copy(source, target, in_sems.at[at])
         for at, (source, target) in enumerate(
-            [(vol_ref, vol_in), (ctl_ref, ctl_in), (sens_ref, sens_in)]
+            [
+                (vol_ref, vol_in),
+                (ctl_ref, ctl_in),
+                (sens_ref, sens_in),
+                (listed_ref, list_ref),
+            ]
         )
     ]
     for copy in inputs:
         copy.start()
-    copies = held_copies(0, inverse_ref, held_refs, rest[10]) if held_count else []
+    copies = held_copies(0, inverse_ref, held_refs, rest[11]) if held_count else []
     for copy in copies:
         copy.start()
 
@@ -205,7 +213,8 @@
         pltpu.VMEM(sens.shape, jnp.float32),
         pltpu.VMEM(vol.shape, jnp.float32),
         pltpu.VMEM(ctl.shape, jnp.float32),
-        pltpu.SemaphoreType.DMA((3,)),
+        pltpu.SMEM(pair_list.shape, jnp.int32),
+        pltpu.SemaphoreType.DMA((4,)),
     ]
     if held_count:
         out_shape += [pltpu.VMEM((PIECE, columns), inverse.dtype)] * held_count
@@ -214,7 +223,7 @@
     return pl.pallas_call(
         functools.partial(pair_kernel, geometry, held_count),
         out_shape=out_shape,
-        in_specs=[smem(), smem(), smem()] + [anywhere()] * 4,
+        in_specs=[smem(), smem()] + [anywhere()] * 5,
         out_specs=out_specs,
         scratch_shapes=scratch,
         compiler_params=pltpu.CompilerParams(vmem_limit_bytes=10 * MIB),
@@ -222,7 +231,12 @@
             flops=512 * 16384 * 400, bytes_accessed=held_count * PIECE * columns * 2, transcendentals=0
         ),
         name="pairs",
-    )(pair_list, pair_count, place, sens, vol, ctl, inverse)
+    )(
+        pair_count,
+        place,
+        *[pltpu.with_memory_space_constraint(x, pltpu.HBM) for x in (pair_list, sens, vol, ctl)],
+        inverse,
+    )
 
 
 def hold_kernel(first, token_ref, inverse_ref, *rest):
@@ -268,10 +282,7 @@
             sems.at[at % slots],
         )
 
-    for at in range(slots):
-        fetch(at).start()
-    yield
-    for at in range(count):
+    def held_part(at):
         value = jnp.zeros((2 * ROWS, chunk), jnp.float32)
         for piece, held_ref in enumerate(held_refs):
             value = value + jnp.dot(
@@ -279,8 +290,16 @@
                 held_ref[:, columns_of(at)],
                 preferred_element_type=jnp.float32,
             )
-        partial[at] = value[:ROWS]
+        partial[at % (AHEAD + 1)] = value[:ROWS]
+
+    for at in range(slots):
+        fetch(at).start()
+    yield
+    for at in range(AHEAD):
+        held_part(at)
     for at in range(count):
+        if at + AHEAD < count:
+            held_part(at + AHEAD)
         fetch(at).wait()
         value = jnp.dot(
             row_loads[:, held:], ring[at % slots], preferred_element_type=jnp.float32
@@ -289,9 +308,9 @@
             fetch(at + slots).start()
         out_ref = out_refs[at // per_out]
         place = at % per_out
-        out_ref[:, place * chunk : (place + 1) * chunk] = (partial[at] + value[:ROWS]).astype(
-            out_ref.dtype
-        )
+        out_ref[:, place * chunk : (place + 1) * chunk] = (
+            partial[at % (AHEAD + 1)] + value[:ROWS]
+        ).astype(out_ref.dtype)
     yield
 
 
@@ -365,7 +384,7 @@
         in_specs=[smem()] + [vmem()] * (len(small) - 1 + len(held)) + [anywhere()],
         out_specs=[vmem()] * len(outs),
         scratch_shapes=[
-            pltpu.VMEM((len(orders), ROWS, chunk), jnp.float32),
+            pltpu.VMEM((AHEAD + 1, ROWS, chunk), jnp.float32),
             pltpu.VMEM((slots, streamed, chunk), inverse.dtype),
             pltpu.SemaphoreType.DMA((slots,)),
         ],
@@ -457,7 +476,8 @@
     spill_a = lax.ppermute(spill, both, cross[0])
     far_same = lax.ppermute(far, "wide", [straight[1](at) for at in spans])
     far_cross = lax.ppermute(far, both, cross[1])
-    held += hold_stage(HELD, MORE, far, inverse)
+    if MORE:
+        held += hold_stage(HELD, MORE, far, inverse)
 
     ends = range(wide // 4)
     quarter = columns // 4

time: 74.4 us -> 70.5 us (0.948)
  local copies, waits for them, and re-layouts: 3.59 us -> 0.01 us
  waiting for transfers between devices: 5.24 us -> 8.68 us
  starting transfers between devices: 33.5 us -> 31.1 us
  Pallas kernels: 31.4 us -> 30.6 us
    pallas_call x1, Pallas kernels: 11.4 us -> 16.8 us  [pair_stage(): pl.pallas_call(functools.partial(pair_kernel, geometry, held_count), out_...]
    unnamed x8 -> x0, local copies, waits for them, and re-layouts: 3.58 us -> none
    pallas_call x1 -> x0, Pallas kernels: 3.39 us -> none  [hold_stage(): pl.pallas_call(functools.partial(hold_kernel, first), out_shape=[pltpu.VM...]
    ppermute x6, starting transfers between devices: 24.9 us -> 22 us  [to(): return lax.ppermute(value, 'wide', [(at, at ^ difference) for at in spans])]
    pallas_call x2, Pallas kernels: 16.6 us -> 13.8 us  [product_stage(): pl.pallas_call(kernel, out_shape=outs, in_specs=[smem()] + [vmem()] * (le...]
    ppermute x1, starting transfers between devices: 3.03 us -> 5.33 us  [local(): partner = lax.ppermute(own, 'narrow', [(0, 1), (1, 0)])]
    ppermute x1, waiting for transfers between devices: 0.76 us -> 2.65 us  [local(): far_same = lax.ppermute(far, 'wide', [straight[1](at) for at in spans])]
    ppermute x1, waiting for transfers between devices: 0.01 us -> 1.85 us  [local(): far_cross = lax.ppermute(far, both, cross[1])]
  transfers between devices with their start and end apart: 11 -> 11, of which waited for: 4 -> 5; matrix products, arithmetic and copies ran while one was open for 0% -> 0% of each run, Pallas kernels for 11% -> 7%
where the time goes in v3:
time: 70.5 us; the launch traced here: 71.8 us
  starting transfers between devices  31.1 us (44%)
  Pallas kernels  30.6 us (43%)
  waiting for transfers between devices  8.68 us (12%)
  other arithmetic  0.74 us (1%)
  between operations  0.74 us (1%)
    ppermute x6, starting transfers between devices, to(): return lax.ppermute(value, 'wide', [(at, at ^ difference) for at in spans])  22 us
    pallas_call x1, Pallas kernels, pair_stage(): pl.pallas_call(functools.partial(pair_kernel, geometry, held_count), out_...  16.8 us
    pallas_call x2, Pallas kernels, product_stage(): pl.pallas_call(kernel, out_shape=outs, in_specs=[smem()] + [vmem()] * (le...  13.8 us
    ppermute x1, starting transfers between devices, local(): partner = lax.ppermute(own, 'narrow', [(0, 1), (1, 0)])  5.33 us
    ppermute x6, waiting for transfers between devices, to(): return lax.ppermute(value, 'wide', [(at, at ^ difference) for at in spans])  4.17 us
    ppermute x1, starting transfers between devices, local(): far_cross = lax.ppermute(far, both, cross[1])  3.55 us
    ppermute x1, waiting for transfers between devices, local(): far_same = lax.ppermute(far, 'wide', [straight[1](at) for at in spans])  2.65 us
    ppermute x1, waiting for transfers between devices, local(): far_cross = lax.ppermute(far, both, cross[1])  1.85 us
  transfers between devices with their start and end apart: 11, of which 5 were waited for; matrix products, arithmetic and copies ran while one was open for 0% of the time, Pallas kernels for 7%

profile of v3, /device:TPU:0, one launch (start us, length us, event | category | flops | bytes accessed | tf_op | source)
XLA Modules:
  0.0 71.8 jit_solution(2381040487471380693)
XLA Ops:
  0.7 0.1 pad_add_fusion.place_ref
  0.7 16.8 %pairs.1 = (f32[16,8,128]{2,1,0:T(8,128)S(1)}, f32[8,8,128]{2,1,0:T(8,128)S(1)}, f32[1,8,128]{2,1,0:T(8,128)S(1)}, bf16[256,16384]{1,0:T(8,128)(2,1)S(1)}, bf16[...) custom-call(s32[1]{0:T(128)S(6)} %copy.7.count_ref, ...), custom_call_target="tpu_custom_call" | custom-call | flops 3355443200 | bytes 41943040 | tf_op jit(solution)/shard_map/pairs/pallas_call | solution.py:223
  17.6 5.3 %collective-permute-start = (f32[16,8,128]{2,1,0:T(8,128)S(1)}, f32[16,8,128]{2,1,0:T(8,128)S(1)}, u32[]{:S(2)}, u32[]{:S(2)}) collective-permute-start(f32[16,8,128]{2,1,0:T(8,128)S(1)} %get-tuple-element.17.own_ref), channel_id=1, source_target_pairs={{0,1},{1,0},{2,3},{3,2},{4,5},{5,4},{6,7},{7,6},{8,9},{9,8},{10,11... | collective-permute-start | bytes 196616 | tf_op jit(solution)/shard_map/ppermute | solution.py:463
  22.9 0.0 collective-permute-start.2
  22.9 0.2 collective-permute-start.1
  23.1 3.5 %collective-permute-start.4 = (f32[1,8,128]{2,1,0:T(8,128)S(1)}, f32[1,8,128]{2,1,0:T(8,128)S(1)}, u32[]{:S(2)}, u32[]{:S(2)}) collective-permute-start(f32[1,8,128]{2,1,0:T(8,128)S(1)} %get-tuple-element.19), channel_id=1, source_target_pairs={{0,17},{1,16},{2,19},{3,18},{4,21},{5,20},{6,23},{7,22},{8,25},{9,... | collective-permute-start | bytes 12296 | tf_op jit(solution)/shard_map/ppermute | solution.py:478
  26.6 0.0 collective-permute-start.3
  26.6 1.9 %collective-permute-done.4.far_cross_ref = f32[1,8,128]{2,1,0:T(8,128)S(1)} collective-permute-done((f32[1,8,128]{2,1,0:T(8,128)S(1)}, f32[1,8,128]{2,1,0:T(8,128)S(1)}, u32[]{:S(2)}, u32[]{:S(2)}) %collective-permute-start.4) | collective-permute-done | bytes 4128 | tf_op jit(solution)/shard_map/ppermute | solution.py:478
  28.5 2.7 %collective-permute-done.3.far_same_ref = f32[1,8,128]{2,1,0:T(8,128)S(1)} collective-permute-done((f32[1,8,128]{2,1,0:T(8,128)S(1)}, f32[1,8,128]{2,1,0:T(8,128)S(1)}, u32[]{:S(2)}, u32[]{:S(2)}) %collective-permute-start.3) | collective-permute-done | bytes 4128 | tf_op jit(solution)/shard_map/ppermute | solution.py:477
  31.1 0.0 collective-permute-done.2.spill_b_ref
  31.1 0.0 collective-permute-done.1.spill_a_ref
  31.1 0.0 collective-permute-done.partner_ref
  31.2 9.1 %product_a.1 = (bf16[16,2048]{1,0:T(8,128)(2,1)S(1)}, bf16[8,4096]{1,0:T(8,128)(2,1)S(1)}, bf16[8,4096]{1,0:T(8,128)(2,1)S(1)}, f32[8,4096]{1,0:T(8,128)S(1)}) custom-call(s32[4]{0:T(128)S(1)} %pad_add_fusion.place_ref, f32[16,8,128]{2,1,0:T(8,128)S(1)} %get-tuple-element.17.own_ref, f32[16,8,128]{2,1,0:T(8,128)S(1)} %collective-permute-done.partner_ref, ...), custom_call_target="tpu_custom_call" | custom-call | flops 402653184 | bytes 25165824 | tf_op jit(solution)/shard_map/product_a/pallas_call | solution.py:381
  40.2 0.1 collective-permute-start.5
  40.3 0.7 collective-permute-start.6
  41.0 1.5 %collective-permute-start.7 = (bf16[8,4096]{1,0:T(8,128)(2,1)S(1)}, bf16[8,4096]{1,0:T(8,128)(2,1)S(1)}, u32[]{:S(2)}, u32[]{:S(2)}) collective-permute-start(bf16[8,4096]{1,0:T(8,128)(2,1)S(1)} %get-tuple-element.28), channel_id=1, source_target_pairs={{0,4},{2,6},{4,0},{6,2},{8,12},{10,14},{12,8},{14,10},{16,20},{18,... | collective-permute-start | bytes 196616 | tf_op jit(solution)/shard_map/ppermute | solution.py:506
  42.5 4.7 %product_b.1 = f32[8,4096]{1,0:T(8,128)S(1)} custom-call(s32[4]{0:T(128)S(1)} %pad_add_fusion.place_ref, bf16[16,2048]{1,0:T(8,128)(2,1)S(1)} %get-tuple-element.25.row_loads, bf16[256,16384]{1,0:T(8,128)(2,1)S(1)} %get-tuple-element.20.rest_0_, bf16[256,16384]{1,0:T(8,128)(2,1)S(1)} %get-tuple-element.21.rest_1_, ...), custom_call_target="tpu_custom_call" | custom-call | flops 134217728 | bytes 8388608 | tf_op jit(solution)/shard_map/product_b/pallas_call | solution.py:381
  47.1 0.0 collective-permute-done.6
  47.2 0.0 collective-permute-done.7
  47.2 0.0 collective-permute-done.5
  47.2 18.3 %collective-permute-start.8 = (bf16[8,1024]{1,0:T(8,128)(2,1)S(1)}, bf16[8,1024]{1,0:T(8,128)(2,1)S(1)}, u32[]{:S(2)}, u32[]{:S(2)}) collective-permute-start(bf16[8,1024]{1,0:T(8,128)(2,1)S(1)} %get-tuple-element.31), channel_id=1, source_target_pairs={{0,8},{2,10},{4,12},{6,14},{8,0},{10,2},{12,4},{14,6},{16,24},{18,... | collective-permute-start | bytes 49160 | tf_op jit(solution)/shard_map/ppermute | solution.py:506
  65.5 0.9 %collective-permute-start.10 = (bf16[8,1024]{1,0:T(8,128)(2,1)S(1)}, bf16[8,1024]{1,0:T(8,128)(2,1)S(1)}, u32[]{:S(2)}, u32[]{:S(2)}) collective-permute-start(bf16[8,1024]{1,0:T(8,128)(2,1)S(1)} %get-tuple-element.32), channel_id=1, source_target_pairs={{0,24},{2,26},{4,28},{6,30},{8,16},{10,18},{12,20},{14,22},{16,8},... | collective-permute-start | bytes 49160 | tf_op jit(solution)/shard_map/ppermute | solution.py:506
  66.4 0.6 collective-permute-start.9
  67.0 0.2 collective-permute-done.8
  67.2 3.8 %collective-permute-done.10 = bf16[8,1024]{1,0:T(8,128)(2,1)S(1)} collective-permute-done((bf16[8,1024]{1,0:T(8,128)(2,1)S(1)}, bf16[8,1024]{1,0:T(8,128)(2,1)S(1)}, u32[]{:S(2)}, u32[]{:S(2)}) %collective-permute-start.10) | collective-permute-done | bytes 16416 | tf_op jit(solution)/shard_map/ppermute | solution.py:506
  71.0 0.2 collective-permute-done.9
  71.2 0.6 fusion.1
  (3 shorter events, 0.0 us)
Async XLA Ops:
  17.6 13.6 %collective-permute-start = (f32[16,8,128]{2,1,0:T(8,128)S(1)}, f32[16,8,128]{2,1,0:T(8,128)S(1)}, u32[]{:S(2)}, u32[]{:S(2)}) collective-permute-start(f32[16,8,128]{2,1,0:T(8,128)S(1)} %get-tuple-element.17.own_ref), channel_id=1, source_target_pairs={{0,1},{1,0},{2,3},{3,2},{4,5},{5,4},{6,7},{7,6},{8,9},{9,8},{10,11... | collective-permute-start | bytes 196616 | tf_op jit(solution)/shard_map/ppermute | solution.py:463
  22.9 8.2 %collective-permute-start.2 = (f32[8,8,128]{2,1,0:T(8,128)S(1)}, f32[8,8,128]{2,1,0:T(8,128)S(1)}, u32[]{:S(2)}, u32[]{:S(2)}) collective-permute-start(f32[8,8,128]{2,1,0:T(8,128)S(1)} %get-tuple-element.18), channel_id=1, source_target_pairs={{0,2},{2,4},{4,6},{6,8},{8,10},{10,12},{12,14},{14,16},{16,18},{18... | collective-permute-start | bytes 98312 | tf_op jit(solution)/shard_map/ppermute | solution.py:475
  22.9 8.2 %collective-permute-start.1 = (f32[8,8,128]{2,1,0:T(8,128)S(1)}, f32[8,8,128]{2,1,0:T(8,128)S(1)}, u32[]{:S(2)}, u32[]{:S(2)}) collective-permute-start(f32[8,8,128]{2,1,0:T(8,128)S(1)} %get-tuple-element.18), channel_id=1, source_target_pairs={{0,3},{1,2},{2,5},{3,4},{4,7},{5,6},{6,9},{7,8},{8,11},{9,10},{10,... | collective-permute-start | bytes 98312 | tf_op jit(solution)/shard_map/ppermute | solution.py:476
  23.1 5.4 %collective-permute-start.4 = (f32[1,8,128]{2,1,0:T(8,128)S(1)}, f32[1,8,128]{2,1,0:T(8,128)S(1)}, u32[]{:S(2)}, u32[]{:S(2)}) collective-permute-start(f32[1,8,128]{2,1,0:T(8,128)S(1)} %get-tuple-element.19), channel_id=1, source_target_pairs={{0,17},{1,16},{2,19},{3,18},{4,21},{5,20},{6,23},{7,22},{8,25},{9,... | collective-permute-start | bytes 12296 | tf_op jit(solution)/shard_map/ppermute | solution.py:478
  26.6 4.5 %collective-permute-start.3 = (f32[1,8,128]{2,1,0:T(8,128)S(1)}, f32[1,8,128]{2,1,0:T(8,128)S(1)}, u32[]{:S(2)}, u32[]{:S(2)}) collective-permute-start(f32[1,8,128]{2,1,0:T(8,128)S(1)} %get-tuple-element.19), channel_id=1, source_target_pairs={{0,16},{2,18},{4,20},{6,22},{8,24},{10,26},{12,28},{14,30},{16,0},... | collective-permute-start | bytes 12296 | tf_op jit(solution)/shard_map/ppermute | solution.py:477
  40.2 6.9 %collective-permute-start.5 = (f32[8,4096]{1,0:T(8,128)S(1)}, f32[8,4096]{1,0:T(8,128)S(1)}, u32[]{:S(2)}, u32[]{:S(2)}) collective-permute-start(f32[8,4096]{1,0:T(8,128)S(1)} %get-tuple-element.26), channel_id=1, source_target_pairs={{0,2},{2,0},{4,6},{6,4},{8,10},{10,8},{12,14},{14,12},{16,18},{18,... | collective-permute-start | bytes 393224 | tf_op jit(solution)/shard_map/ppermute | solution.py:506
  40.3 6.8 %collective-permute-start.6 = (bf16[8,4096]{1,0:T(8,128)(2,1)S(1)}, bf16[8,4096]{1,0:T(8,128)(2,1)S(1)}, u32[]{:S(2)}, u32[]{:S(2)}) collective-permute-start(bf16[8,4096]{1,0:T(8,128)(2,1)S(1)} %get-tuple-element.27), channel_id=1, source_target_pairs={{0,6},{2,4},{4,2},{6,0},{8,14},{10,12},{12,10},{14,8},{16,22},{18,... | collective-permute-start | bytes 196616 | tf_op jit(solution)/shard_map/ppermute | solution.py:506
  41.0 6.2 %collective-permute-start.7 = (bf16[8,4096]{1,0:T(8,128)(2,1)S(1)}, bf16[8,4096]{1,0:T(8,128)(2,1)S(1)}, u32[]{:S(2)}, u32[]{:S(2)}) collective-permute-start(bf16[8,4096]{1,0:T(8,128)(2,1)S(1)} %get-tuple-element.28), channel_id=1, source_target_pairs={{0,4},{2,6},{4,0},{6,2},{8,12},{10,14},{12,8},{14,10},{16,20},{18,... | collective-permute-start | bytes 196616 | tf_op jit(solution)/shard_map/ppermute | solution.py:506
  47.2 20.0 %collective-permute-start.8 = (bf16[8,1024]{1,0:T(8,128)(2,1)S(1)}, bf16[8,1024]{1,0:T(8,128)(2,1)S(1)}, u32[]{:S(2)}, u32[]{:S(2)}) collective-permute-start(bf16[8,1024]{1,0:T(8,128)(2,1)S(1)} %get-tuple-element.31), channel_id=1, source_target_pairs={{0,8},{2,10},{4,12},{6,14},{8,0},{10,2},{12,4},{14,6},{16,24},{18,... | collective-permute-start | bytes 49160 | tf_op jit(solution)/shard_map/ppermute | solution.py:506
  65.5 5.5 %collective-permute-start.10 = (bf16[8,1024]{1,0:T(8,128)(2,1)S(1)}, bf16[8,1024]{1,0:T(8,128)(2,1)S(1)}, u32[]{:S(2)}, u32[]{:S(2)}) collective-permute-start(bf16[8,1024]{1,0:T(8,128)(2,1)S(1)} %get-tuple-element.32), channel_id=1, source_target_pairs={{0,24},{2,26},{4,28},{6,30},{8,16},{10,18},{12,20},{14,22},{16,8},... | collective-permute-start | bytes 49160 | tf_op jit(solution)/shard_map/ppermute | solution.py:506
  66.4 4.8 %collective-permute-start.9 = (bf16[8,1024]{1,0:T(8,128)(2,1)S(1)}, bf16[8,1024]{1,0:T(8,128)(2,1)S(1)}, u32[]{:S(2)}, u32[]{:S(2)}) collective-permute-start(bf16[8,1024]{1,0:T(8,128)(2,1)S(1)} %get-tuple-element.33), channel_id=1, source_target_pairs={{0,16},{2,18},{4,20},{6,22},{8,24},{10,26},{12,28},{14,30},{16,0},... | collective-permute-start | bytes 49160 | tf_op jit(solution)/shard_map/ppermute | solution.py:506

commit v4 on v3

--- a/solution.py
+++ b/solution.py
@@ -16,9 +16,8 @@
 DEPTH = 64
 MIB = 1 << 20
 PIECE = 256
-HELD = 5
-MORE = 0
-SLOTS = 4
+HELD = 4
+SLOTS = 3
 PRODUCT_MIB = 7
 
 
@@ -54,18 +53,36 @@
     return jnp.concatenate(parts, axis=0)
 
 
-def held_copies(first, inverse_ref, held_refs, sems):
-    return [
-        pltpu.make_async_copy(
-            inverse_ref.at[pl.ds((first + at) * PIECE, PIECE), :], held_ref, sems.at[at]
-        )
-        for at, held_ref in enumerate(held_refs)
-    ]
+def chunk_start(me, near, far, chunk):
+    return pl.multiple_of((me ^ (near | (far << 2))) * chunk, chunk)
+
+
+def held_copies(me, inverse_ref, held_refs, near_refs, sems=None):
+    copies = []
+    for at, held_ref in enumerate(held_refs):
+        rows = pl.ds(at * PIECE, PIECE)
+        copies.append(pltpu.make_async_copy(inverse_ref.at[rows, :], held_ref, sems.at[at]))
+    for near_ref in near_refs:
+        depth, width = near_ref.shape
+        rows = pl.ds(len(held_refs) * PIECE, depth)
+        pieces = sems.shape[0] - len(held_refs)
+        chunk = width // pieces
+        for at in range(pieces):
+            columns = pl.ds(chunk_start(me, 0, at, chunk), chunk)
+            copies.append(
+                pltpu.make_async_copy(
+                    inverse_ref.at[rows, columns],
+                    near_ref.at[:, pl.ds(at * chunk, chunk)],
+                    sems.at[len(held_refs) + at],
+                )
+            )
+    return copies
 
 
 def pair_kernel(
     geometry,
     held_count,
+    near_count,
     count_ref,
     place_ref,
     listed_ref,
@@ -80,6 +97,7 @@
 ):
     ctiles, tpb, tiles = geometry
     held_refs, rest = rest[:held_count], rest[held_count:]
+    near_refs, rest = rest[:near_count], rest[near_count:]
     nodes, points, weights, loads_ref, squares, kernels, sens_in, vol_in, ctl_in, list_ref, in_sems = (
         rest[:11]
     )
@@ -98,9 +116,7 @@
     ]
     for copy in inputs:
         copy.start()
-    copies = held_copies(0, inverse_ref, held_refs, rest[11]) if held_count else []
-    for copy in copies:
-        copy.start()
+    copies = held_copies(place_ref[2], inverse_ref, held_refs, near_refs, *rest[11:])
 
     first_tile = place_ref[0]
     far_tile = place_ref[1]
@@ -111,12 +127,17 @@
     weights[vtiles] = jnp.zeros(weights.shape[1:], jnp.bfloat16)
     for copy in inputs:
         copy.wait()
+    for copy in copies:
+        copy.start()
 
     group = 8
+    square = (VT, VT)
+    same = lax.broadcasted_iota(jnp.int32, square, 0) == lax.broadcasted_iota(jnp.int32, square, 1)
+    unit = jnp.where(same, 1.0, 0.0).astype(jnp.bfloat16)
 
     def node_group(group_id, carry):
         begin = pl.multiple_of(group_id * (group * VT), group * VT)
-        rows = features(vol_in[:, pl.ds(begin, group * VT)], True)
+        rows = features(vol_in[:, pl.ds(begin, group * VT)], True).astype(jnp.bfloat16)
         sens = sens_in[:, pl.ds(begin, group * VT)]
         components = sens.shape[0]
         if components < ROWS:
@@ -127,7 +148,10 @@
         both = jnp.concatenate([high, sens - high], axis=0).astype(jnp.bfloat16)
         for at in range(group):
             cut = slice(at * VT, (at + 1) * VT)
-            nodes[group_id * group + at] = rows[:, cut].T.astype(jnp.bfloat16)
+            turned = lax.dot_general(
+                unit, rows[:, cut], (((1,), (1,)), ((), ())), preferred_element_type=jnp.float32
+            )
+            nodes[group_id * group + at] = turned.astype(jnp.bfloat16)
             weights[group_id * group + at] = jnp.concatenate([both[:, cut], both[:, cut]], axis=1)
         return carry
 
@@ -157,7 +181,6 @@
             weight = weights[jnp.where(live, volume, vtiles)]
             terms = jnp.dot(weight, kernels[at], preferred_element_type=jnp.float32)
             results.append((control, terms[:ROWS] + terms[ROWS:]))
-        for at in range(UNROLL):
             squared = jnp.maximum(squares[at], 1e-12)
             radius = squared * lax.rsqrt(squared)
             inside = jnp.maximum(4.0 - radius, 0.0)
@@ -166,7 +189,6 @@
             high = kernel.astype(jnp.bfloat16)
             kernels[at, :VT] = high
             kernels[at, VT:] = (kernel - high.astype(jnp.float32)).astype(jnp.bfloat16)
-        for at in range(UNROLL):
             _, volume, control = tiles_of(step_id * UNROLL + at)
             squares[at] = jnp.dot(
                 nodes[volume], points[control], preferred_element_type=jnp.float32
@@ -195,7 +217,7 @@
     return pl.BlockSpec(memory_space=pltpu.HBM)
 
 
-def pair_stage(geometry, held_count, pair_list, pair_count, place, sens, vol, ctl, inverse):
+def pair_stage(geometry, held_count, near_shape, pair_list, pair_count, place, sens, vol, ctl, inverse):
     ctiles, tpb, tiles = geometry
     vtiles = vol.shape[1] // VT
     columns = inverse.shape[1]
@@ -219,9 +241,12 @@
     if held_count:
         out_shape += [pltpu.VMEM((PIECE, columns), inverse.dtype)] * held_count
         out_specs += [vmem()] * held_count
-        scratch.append(pltpu.SemaphoreType.DMA((held_count,)))
+        pieces, depth, width = near_shape
+        out_shape.append(pltpu.VMEM((depth, pieces * width), inverse.dtype))
+        out_specs.append(vmem())
+        scratch.append(pltpu.SemaphoreType.DMA((held_count + pieces,)))
     return pl.pallas_call(
-        functools.partial(pair_kernel, geometry, held_count),
+        functools.partial(pair_kernel, geometry, held_count, 1 if held_count else 0),
         out_shape=out_shape,
         in_specs=[smem(), smem()] + [anywhere()] * 5,
         out_specs=out_specs,
@@ -239,41 +264,25 @@
     )
 
 
-def hold_kernel(first, token_ref, inverse_ref, *rest):
-    del token_ref
-    copies = held_copies(first, inverse_ref, rest[:-1], rest[-1])
-    for copy in copies:
-        copy.start()
-    for copy in copies:
-        copy.wait()
-
-
-def hold_stage(first, count, token, inverse):
-    columns = inverse.shape[1]
-    return pl.pallas_call(
-        functools.partial(hold_kernel, first),
-        out_shape=[pltpu.VMEM((PIECE, columns), inverse.dtype)] * count,
-        in_specs=[anywhere(), anywhere()],
-        out_specs=[vmem()] * count,
-        scratch_shapes=[pltpu.SemaphoreType.DMA((count,))],
-        compiler_params=pltpu.CompilerParams(vmem_limit_bytes=1 * MIB),
-        cost_estimate=pl.CostEstimate(
-            flops=0, bytes_accessed=2 * count * PIECE * columns * 2, transcendentals=0
-        ),
-        name="hold",
-    )(token, inverse)
+def held_part(row_loads, held_refs, columns):
+    value = jnp.zeros((2 * ROWS, columns.size), jnp.float32)
+    for piece, held_ref in enumerate(held_refs):
+        value = value + jnp.dot(
+            row_loads[:, piece * PIECE : (piece + 1) * PIECE],
+            held_ref[:, columns],
+            preferred_element_type=jnp.float32,
+        )
+    return value[:ROWS]
 
 
 def multiply(orders, me, row_loads, held_refs, inverse_ref, out_refs, partial, ring, sems):
-    streamed = ring.shape[1]
+    slots, streamed, chunk = ring.shape
     held = inverse_ref.shape[0] - streamed
-    chunk = ring.shape[2]
-    slots = ring.shape[0]
     count = len(orders)
     per_out = count // len(out_refs)
 
     def columns_of(at):
-        return pl.ds(pl.multiple_of((me ^ orders[at]) * chunk, chunk), chunk)
+        return pl.ds(chunk_start(me, *orders[at], chunk), chunk)
 
     def fetch(at):
         return pltpu.make_async_copy(
@@ -282,24 +291,16 @@
             sems.at[at % slots],
         )
 
-    def held_part(at):
-        value = jnp.zeros((2 * ROWS, chunk), jnp.float32)
-        for piece, held_ref in enumerate(held_refs):
-            value = value + jnp.dot(
-                row_loads[:, piece * PIECE : (piece + 1) * PIECE],
-                held_ref[:, columns_of(at)],
-                preferred_element_type=jnp.float32,
-            )
-        partial[at % (AHEAD + 1)] = value[:ROWS]
-
     for at in range(slots):
         fetch(at).start()
     yield
     for at in range(AHEAD):
-        held_part(at)
+        partial[at] = held_part(row_loads, held_refs, columns_of(at))
     for at in range(count):
         if at + AHEAD < count:
-            held_part(at + AHEAD)
+            partial[(at + AHEAD) % (AHEAD + 1)] = held_part(
+                row_loads, held_refs, columns_of(at + AHEAD)
+            )
         fetch(at).wait()
         value = jnp.dot(
             row_loads[:, held:], ring[at % slots], preferred_element_type=jnp.float32
@@ -326,8 +327,8 @@
     far_cross_ref,
     *rest,
 ):
-    held_refs = rest[:-8]
-    inverse_ref, row_loads, *out_refs, partial, ring, sems = rest[-8:]
+    held_refs = rest[:-9]
+    _, inverse_ref, row_loads, *out_refs, partial, ring, sems = rest[-9:]
     tpb = partner_ref.shape[0]
     spilled = spill_a_ref.shape[0]
     even = place_ref[3] == 0
@@ -356,50 +357,33 @@
     next(steps)
 
 
-def next_kernel(orders, place_ref, row_loads, *rest):
-    held_refs = rest[:-5]
-    inverse_ref, out_ref, partial, ring, sems = rest[-5:]
-    steps = multiply(
-        orders,
-        place_ref[2],
-        row_loads,
-        held_refs,
-        inverse_ref,
-        [out_ref],
-        partial,
-        ring,
-        sems,
-    )
-    next(steps)
-    next(steps)
-
-
-def product_stage(kernel, orders, chunk, small, held, inverse, outs, name):
-    rows = inverse.shape[0]
-    streamed = rows - len(held) * PIECE
-    slots = min(SLOTS, len(orders))
+def near_kernel(count, place_ref, row_loads, *rest):
+    *held_refs, near_ref, out_ref = rest
+    held = len(held_refs) * PIECE
+    chunk = near_ref.shape[1] // count
+    for at in range(count):
+        place = slice(at * chunk, (at + 1) * chunk)
+        columns = pl.ds(chunk_start(place_ref[2], 0, at, chunk), chunk)
+        value = held_part(row_loads, held_refs, columns)
+        value = value + jnp.dot(
+            row_loads[:, held:], near_ref[:, place], preferred_element_type=jnp.float32
+        )[:ROWS]
+        out_ref[:, place] = value
+
+
+def product_stage(kernel, small, pinned, rest, outs, scratch, name):
     return pl.pallas_call(
         kernel,
         out_shape=outs,
-        in_specs=[smem()] + [vmem()] * (len(small) - 1 + len(held)) + [anywhere()],
+        in_specs=[smem()] + [vmem()] * (len(small) - 1 + len(pinned)) + [anywhere()] * len(rest),
         out_specs=[vmem()] * len(outs),
-        scratch_shapes=[
-            pltpu.VMEM((AHEAD + 1, ROWS, chunk), jnp.float32),
-            pltpu.VMEM((slots, streamed, chunk), inverse.dtype),
-            pltpu.SemaphoreType.DMA((slots,)),
-        ],
+        scratch_shapes=scratch,
         compiler_params=pltpu.CompilerParams(vmem_limit_bytes=PRODUCT_MIB * MIB),
         cost_estimate=pl.CostEstimate(
-            flops=16 * rows * chunk * len(orders),
-            bytes_accessed=rows * chunk * len(orders),
-            transcendentals=0,
+            flops=16 * 2048 * 4096, bytes_accessed=16 * MIB, transcendentals=0
         ),
         name=name,
-    )(
-        *small,
-        *[pltpu.with_memory_space_constraint(piece, pltpu.VMEM) for piece in held],
-        inverse,
-    )
+    )(*small, *[pltpu.with_memory_space_constraint(piece, pltpu.VMEM) for piece in pinned], *rest)
 
 
 def local(wide, narrow, sensitivity, vol_coord, ctl_coord, pair_list, pair_count, inverse):
@@ -432,7 +416,7 @@
     )
     if not fast:
         own, spill, far_tile_loads = pair_stage(
-            geometry, 0, pair_list, pair_count, place, sensitivity, vol_coord, ctl_coord, inverse
+            geometry, 0, (), pair_list, pair_count, place, sensitivity, vol_coord, ctl_coord, inverse
         )
         spans = -(-tiles // tpb)
         band = jnp.pad(spill, ((0, spans * tpb - tiles), (0, 0), (0, 0)))
@@ -456,9 +440,21 @@
         )
         return lax.psum_scatter(terms, "wide", scatter_dimension=1, tiled=True)
 
-    own, spill, far, *held = pair_stage(
-        geometry, HELD, pair_list, pair_count, place, sensitivity, vol_coord, ctl_coord, inverse
-    )
+    ends = range(wide // 4)
+    streamed = row_count - HELD * PIECE
+    own, spill, far, *pinned = pair_stage(
+        geometry,
+        HELD,
+        (len(ends), streamed, chunk),
+        pair_list,
+        pair_count,
+        place,
+        sensitivity,
+        vol_coord,
+        ctl_coord,
+        inverse,
+    )
+    held, near = pinned[:HELD], pinned[HELD:]
     both = ("wide", "narrow")
     partner = lax.ppermute(own, "narrow", [(0, 1), (1, 0)])
 
@@ -476,54 +472,47 @@
     spill_a = lax.ppermute(spill, both, cross[0])
     far_same = lax.ppermute(far, "wide", [straight[1](at) for at in spans])
     far_cross = lax.ppermute(far, both, cross[1])
-    if MORE:
-        held += hold_stage(HELD, MORE, far, inverse)
-
-    ends = range(wide // 4)
     quarter = columns // 4
-
-    def orders_of(near):
-        return [near | (end << 2) for end in ends]
-
-    orders = orders_of(3) + orders_of(2) + orders_of(1)
-    row_loads, part_3, part_2, part_1 = product_stage(
+    orders = [(difference, end) for difference in (3, 2, 1) for end in ends]
+    parts = product_stage(
         functools.partial(first_kernel, orders, offsets),
-        orders,
-        chunk,
         [place, own, partner, spill_a, spill_b, far_same, far_cross],
-        held,
-        inverse,
+        held + near,
+        [inverse],
         [
             pltpu.VMEM((2 * ROWS, row_count), jnp.bfloat16),
             jax.ShapeDtypeStruct((ROWS, quarter), jnp.bfloat16),
             jax.ShapeDtypeStruct((ROWS, quarter), jnp.bfloat16),
             jax.ShapeDtypeStruct((ROWS, quarter), jnp.float32),
         ],
+        [
+            pltpu.VMEM((AHEAD + 1, ROWS, chunk), jnp.float32),
+            pltpu.VMEM((SLOTS, streamed, chunk), inverse.dtype),
+            pltpu.SemaphoreType.DMA((SLOTS,)),
+        ],
         "product_a",
     )
-
-    def to(difference, value):
-        return lax.ppermute(value, "wide", [(at, at ^ difference) for at in spans])
-
-    part_3 = to(3, part_3)
-    part_2 = to(2, part_2)
-    part_1 = to(1, part_1)
-    orders = orders_of(0)
-    (part_0,) = product_stage(
-        functools.partial(next_kernel, orders),
-        orders,
-        chunk,
+    row_loads = parts[0]
+    moved = [
+        lax.ppermute(part, "wide", [(at, at ^ difference) for at in spans])
+        for part, difference in zip(parts[1:], (3, 2, 1))
+    ]
+    (total,) = product_stage(
+        functools.partial(near_kernel, len(ends)),
         [place, row_loads],
-        held,
-        inverse,
+        held + near,
+        [],
         [jax.ShapeDtypeStruct((ROWS, quarter), jnp.float32)],
+        [],
         "product_b",
     )
-    total = part_0 + part_1 + part_3.astype(jnp.float32) + part_2.astype(jnp.float32)
+    for part in moved:
+        total = total + part.astype(jnp.float32)
     result = total[:, :chunk]
     for end in ends[1:]:
         sent = total[:, end * chunk : (end + 1) * chunk].astype(jnp.bfloat16)
-        result = result + to(end << 2, sent).astype(jnp.float32)
+        got = lax.ppermute(sent, "wide", [(at, at ^ (end << 2)) for at in spans])
+        result = result + got.astype(jnp.float32)
     return result[:components]
 
 

time: 70.5 us -> 63 us (0.89); the launches traced: 71.8 us -> 61.9 us
  starting transfers between devices: 31.1 us -> 22.4 us
  Pallas kernels: 30.6 us -> 28.3 us
  waiting for transfers between devices: 8.68 us -> 9.69 us
    ppermute x6, starting transfers between devices: 22 us -> 13.8 us  [the longest x3 10.2 us: local(): lax.ppermute(part, 'wide', [(at, at ^ difference) for at in spans])]
    ppermute x1, starting transfers between devices: 5.33 us -> 3.03 us  [local(): partner = lax.ppermute(own, 'narrow', [(0, 1), (1, 0)])]
    pallas_call x1, Pallas kernels: 16.8 us -> 14.8 us  [pair_stage(): pl.pallas_call(functools.partial(pair_kernel, geometry, held_count, 1 if...]
    ppermute x1, starting transfers between devices: 0.17 us -> 1.71 us  [local(): spill_a = lax.ppermute(spill, both, cross[0])]
    ppermute x6, waiting for transfers between devices: 4.17 us -> 5.51 us  [the longest x3 4.23 us: local(): got = lax.ppermute(sent, 'wide', [(at, at ^ end << 2) for at in spans])]
  transfers between devices with their start and end apart: 11 -> 11, of which waited for: 5 -> 6; matrix products, arithmetic and copies ran while one was open for 0% -> 0% of each run, Pallas kernels for 7% -> 5%
where the time goes in v4:
time: 63 us; the launch traced here: 61.9 us
  Pallas kernels  28.3 us (45%)
  starting transfers between devices  22.4 us (36%)
  waiting for transfers between devices  9.69 us (15%)
  other arithmetic  0.74 us (1%)
  between operations  0.71 us (1%)
    pallas_call x1, Pallas kernels, pair_stage(): pl.pallas_call(functools.partial(pair_kernel, geometry, held_count, 1 if...  14.8 us
    pallas_call x2, Pallas kernels, product_stage(): pl.pallas_call(kernel, out_shape=outs, in_specs=[smem()] + [vmem()] * (le...  13.6 us
    ppermute x3, starting transfers between devices, local(): lax.ppermute(part, 'wide', [(at, at ^ difference) for at in spans])  10.2 us
    ppermute x3, waiting for transfers between devices, local(): got = lax.ppermute(sent, 'wide', [(at, at ^ end << 2) for at in spans])  4.23 us
    ppermute x3, starting transfers between devices, local(): got = lax.ppermute(sent, 'wide', [(at, at ^ end << 2) for at in spans])  3.55 us
    ppermute x1, starting transfers between devices, local(): far_cross = lax.ppermute(far, both, cross[1])  3.54 us
    ppermute x1, starting transfers between devices, local(): partner = lax.ppermute(own, 'narrow', [(0, 1), (1, 0)])  3.03 us
    ppermute x1, waiting for transfers between devices, local(): far_same = lax.ppermute(far, 'wide', [straight[1](at) for at in spans])  2.65 us
  transfers between devices with their start and end apart: 11, of which 6 were waited for; matrix products, arithmetic and copies ran while one was open for 0% of the time, Pallas kernels for 5%

profile of v4, /device:TPU:0, one launch (start us, length us, event | category | flops | bytes accessed | tf_op | source)
XLA Modules:
  0.0 61.9 jit_solution(14945357221925945649)
XLA Ops:
  0.7 0.1 pad_add_fusion.place_ref
  0.7 14.8 %pairs.1 = (f32[16,8,128]{2,1,0:T(8,128)S(1)}, f32[8,8,128]{2,1,0:T(8,128)S(1)}, f32[1,8,128]{2,1,0:T(8,128)S(1)}, bf16[256,16384]{1,0:T(8,128)(2,1)S(1)}, bf16[...) custom-call(s32[1]{0:T(128)S(6)} %copy.7.count_ref, ...), custom_call_target="tpu_custom_call" | custom-call | flops 3355443200 | bytes 33554432 | tf_op jit(solution)/shard_map/pairs/pallas_call | solution.py:248
  15.5 3.0 %collective-permute-start = (f32[16,8,128]{2,1,0:T(8,128)S(1)}, f32[16,8,128]{2,1,0:T(8,128)S(1)}, u32[]{:S(2)}, u32[]{:S(2)}) collective-permute-start(f32[16,8,128]{2,1,0:T(8,128)S(1)} %get-tuple-element.17.own_ref), channel_id=1, source_target_pairs={{0,1},{1,0},{2,3},{3,2},{4,5},{5,4},{6,7},{7,6},{8,9},{9,8},{10,11... | collective-permute-start | bytes 196616 | tf_op jit(solution)/shard_map/ppermute | solution.py:459
  18.6 0.0 collective-permute-start.2
  18.6 1.7 %collective-permute-start.1 = (f32[8,8,128]{2,1,0:T(8,128)S(1)}, f32[8,8,128]{2,1,0:T(8,128)S(1)}, u32[]{:S(2)}, u32[]{:S(2)}) collective-permute-start(f32[8,8,128]{2,1,0:T(8,128)S(1)} %get-tuple-element.18), channel_id=1, source_target_pairs={{0,3},{1,2},{2,5},{3,4},{4,7},{5,6},{6,9},{7,8},{8,11},{9,10},{10,... | collective-permute-start | bytes 98312 | tf_op jit(solution)/shard_map/ppermute | solution.py:472
  20.3 3.5 %collective-permute-start.4 = (f32[1,8,128]{2,1,0:T(8,128)S(1)}, f32[1,8,128]{2,1,0:T(8,128)S(1)}, u32[]{:S(2)}, u32[]{:S(2)}) collective-permute-start(f32[1,8,128]{2,1,0:T(8,128)S(1)} %get-tuple-element.19), channel_id=1, source_target_pairs={{0,17},{1,16},{2,19},{3,18},{4,21},{5,20},{6,23},{7,22},{8,25},{9,... | collective-permute-start | bytes 12296 | tf_op jit(solution)/shard_map/ppermute | solution.py:474
  23.8 0.3 collective-permute-start.3
  24.2 1.5 %collective-permute-done.4.far_cross_ref = f32[1,8,128]{2,1,0:T(8,128)S(1)} collective-permute-done((f32[1,8,128]{2,1,0:T(8,128)S(1)}, f32[1,8,128]{2,1,0:T(8,128)S(1)}, u32[]{:S(2)}, u32[]{:S(2)}) %collective-permute-start.4) | collective-permute-done | bytes 4128 | tf_op jit(solution)/shard_map/ppermute | solution.py:474
  25.7 2.6 %collective-permute-done.3.far_same_ref = f32[1,8,128]{2,1,0:T(8,128)S(1)} collective-permute-done((f32[1,8,128]{2,1,0:T(8,128)S(1)}, f32[1,8,128]{2,1,0:T(8,128)S(1)}, u32[]{:S(2)}, u32[]{:S(2)}) %collective-permute-start.3) | collective-permute-done | bytes 4128 | tf_op jit(solution)/shard_map/ppermute | solution.py:473
  28.3 0.0 collective-permute-done.2.spill_b_ref
  28.3 0.0 collective-permute-done.1.spill_a_ref
  28.3 0.0 collective-permute-done.partner_ref
  28.3 10.7 %product_a.1 = (bf16[16,2048]{1,0:T(8,128)(2,1)S(1)}, bf16[8,4096]{1,0:T(8,128)(2,1)S(1)}, bf16[8,4096]{1,0:T(8,128)(2,1)S(1)}, f32[8,4096]{1,0:T(8,128)S(1)}) custom-call(s32[4]{0:T(128)S(1)} %pad_add_fusion.place_ref, f32[16,8,128]{2,1,0:T(8,128)S(1)} %get-tuple-element.17.own_ref, f32[16,8,128]{2,1,0:T(8,128)S(1)} %collective-permute-done.partner_ref, ...), custom_call_target="tpu_custom_call" | custom-call | flops 134217728 | bytes 16777216 | tf_op jit(solution)/shard_map/product_a/pallas_call | solution.py:375
  39.1 0.1 collective-permute-start.7
  39.2 9.8 %collective-permute-start.5 = (bf16[8,4096]{1,0:T(8,128)(2,1)S(1)}, bf16[8,4096]{1,0:T(8,128)(2,1)S(1)}, u32[]{:S(2)}, u32[]{:S(2)}) collective-permute-start(bf16[8,4096]{1,0:T(8,128)(2,1)S(1)} %get-tuple-element.26), channel_id=1, source_target_pairs={{0,6},{2,4},{4,2},{6,0},{8,14},{10,12},{12,10},{14,8},{16,22},{18,... | collective-permute-start | bytes 196616 | tf_op jit(solution)/shard_map/ppermute | solution.py:497
  49.0 0.3 collective-permute-start.6
  49.3 2.8 %product_b.1 = f32[8,4096]{1,0:T(8,128)S(1)} custom-call(s32[4]{0:T(128)S(1)} %pad_add_fusion.place_ref, bf16[16,2048]{1,0:T(8,128)(2,1)S(1)} %get-tuple-element.25.row_loads, bf16[256,16384]{1,0:T(8,128)(2,1)S(1)} %get-tuple-element.20.rest_0_, bf16[256,16384]{1,0:T(8,128)(2,1)S(1)} %get-tuple-element.21.rest_1_, ...), custom_call_target="tpu_custom_call" | custom-call | flops 134217728 | bytes 16777216 | tf_op jit(solution)/shard_map/product_b/pallas_call | solution.py:375
  52.1 0.0 collective-permute-done.5
  52.2 1.3 %collective-permute-done.6 = bf16[8,4096]{1,0:T(8,128)(2,1)S(1)} collective-permute-done((bf16[8,4096]{1,0:T(8,128)(2,1)S(1)}, bf16[8,4096]{1,0:T(8,128)(2,1)S(1)}, u32[]{:S(2)}, u32[]{:S(2)}) %collective-permute-start.6) | collective-permute-done | bytes 65568 | tf_op jit(solution)/shard_map/ppermute | solution.py:497
  53.4 0.0 collective-permute-done.7
  53.5 1.9 %collective-permute-start.8 = (bf16[8,1024]{1,0:T(8,128)(2,1)S(1)}, bf16[8,1024]{1,0:T(8,128)(2,1)S(1)}, u32[]{:S(2)}, u32[]{:S(2)}) collective-permute-start(bf16[8,1024]{1,0:T(8,128)(2,1)S(1)} %get-tuple-element.31), channel_id=1, source_target_pairs={{0,8},{2,10},{4,12},{6,14},{8,0},{10,2},{12,4},{14,6},{16,24},{18,... | collective-permute-start | bytes 49160 | tf_op jit(solution)/shard_map/ppermute | solution.py:514
  55.4 1.0 %collective-permute-start.10 = (bf16[8,1024]{1,0:T(8,128)(2,1)S(1)}, bf16[8,1024]{1,0:T(8,128)(2,1)S(1)}, u32[]{:S(2)}, u32[]{:S(2)}) collective-permute-start(bf16[8,1024]{1,0:T(8,128)(2,1)S(1)} %get-tuple-element.32), channel_id=1, source_target_pairs={{0,24},{2,26},{4,28},{6,30},{8,16},{10,18},{12,20},{14,22},{16,8},... | collective-permute-start | bytes 49160 | tf_op jit(solution)/shard_map/ppermute | solution.py:514
  56.4 0.6 %collective-permute-start.9 = (bf16[8,1024]{1,0:T(8,128)(2,1)S(1)}, bf16[8,1024]{1,0:T(8,128)(2,1)S(1)}, u32[]{:S(2)}, u32[]{:S(2)}) collective-permute-start(bf16[8,1024]{1,0:T(8,128)(2,1)S(1)} %get-tuple-element.33), channel_id=1, source_target_pairs={{0,16},{2,18},{4,20},{6,22},{8,24},{10,26},{12,28},{14,30},{16,0},... | collective-permute-start | bytes 49160 | tf_op jit(solution)/shard_map/ppermute | solution.py:514
  57.1 0.2 collective-permute-done.8
  57.3 3.6 %collective-permute-done.10 = bf16[8,1024]{1,0:T(8,128)(2,1)S(1)} collective-permute-done((bf16[8,1024]{1,0:T(8,128)(2,1)S(1)}, bf16[8,1024]{1,0:T(8,128)(2,1)S(1)}, u32[]{:S(2)}, u32[]{:S(2)}) %collective-permute-start.10) | collective-permute-done | bytes 16416 | tf_op jit(solution)/shard_map/ppermute | solution.py:514
  60.9 0.4 collective-permute-done.9
  61.3 0.6 %fusion.1 = f32[6,1024]{1,0:T(8,128)} fusion(f32[8,1024]{1,0:T(8,128)S(1)} %slice.23, bf16[8,1024]{1,0:T(8,128)(2,1)S(1)} %collective-permute-done.10, bf16[8,1024]{1,0:T(8,128)(2,1)S(1)} %collective-permute-done.9, bf16[8,1024]{1,0:T(8,128)(2,1)S(1)} %collective-permute-done.8), kind=kLoop, calls=%fused_computation.3 | loop fusion | flops 36864 | bytes 86016 | tf_op jit(solution)/shard_map/add | solution.py:515
  (3 shorter events, 0.1 us)
Async XLA Ops:
  15.5 12.8 %collective-permute-start = (f32[16,8,128]{2,1,0:T(8,128)S(1)}, f32[16,8,128]{2,1,0:T(8,128)S(1)}, u32[]{:S(2)}, u32[]{:S(2)}) collective-permute-start(f32[16,8,128]{2,1,0:T(8,128)S(1)} %get-tuple-element.17.own_ref), channel_id=1, source_target_pairs={{0,1},{1,0},{2,3},{3,2},{4,5},{5,4},{6,7},{7,6},{8,9},{9,8},{10,11... | collective-permute-start | bytes 196616 | tf_op jit(solution)/shard_map/ppermute | solution.py:459
  18.6 9.8 %collective-permute-start.2 = (f32[8,8,128]{2,1,0:T(8,128)S(1)}, f32[8,8,128]{2,1,0:T(8,128)S(1)}, u32[]{:S(2)}, u32[]{:S(2)}) collective-permute-start(f32[8,8,128]{2,1,0:T(8,128)S(1)} %get-tuple-element.18), channel_id=1, source_target_pairs={{0,2},{2,4},{4,6},{6,8},{8,10},{10,12},{12,14},{14,16},{16,18},{18... | collective-permute-start | bytes 98312 | tf_op jit(solution)/shard_map/ppermute | solution.py:471
  18.6 9.8 %collective-permute-start.1 = (f32[8,8,128]{2,1,0:T(8,128)S(1)}, f32[8,8,128]{2,1,0:T(8,128)S(1)}, u32[]{:S(2)}, u32[]{:S(2)}) collective-permute-start(f32[8,8,128]{2,1,0:T(8,128)S(1)} %get-tuple-element.18), channel_id=1, source_target_pairs={{0,3},{1,2},{2,5},{3,4},{4,7},{5,6},{6,9},{7,8},{8,11},{9,10},{10,... | collective-permute-start | bytes 98312 | tf_op jit(solution)/shard_map/ppermute | solution.py:472
  20.3 5.4 %collective-permute-start.4 = (f32[1,8,128]{2,1,0:T(8,128)S(1)}, f32[1,8,128]{2,1,0:T(8,128)S(1)}, u32[]{:S(2)}, u32[]{:S(2)}) collective-permute-start(f32[1,8,128]{2,1,0:T(8,128)S(1)} %get-tuple-element.19), channel_id=1, source_target_pairs={{0,17},{1,16},{2,19},{3,18},{4,21},{5,20},{6,23},{7,22},{8,25},{9,... | collective-permute-start | bytes 12296 | tf_op jit(solution)/shard_map/ppermute | solution.py:474
  23.8 4.5 %collective-permute-start.3 = (f32[1,8,128]{2,1,0:T(8,128)S(1)}, f32[1,8,128]{2,1,0:T(8,128)S(1)}, u32[]{:S(2)}, u32[]{:S(2)}) collective-permute-start(f32[1,8,128]{2,1,0:T(8,128)S(1)} %get-tuple-element.19), channel_id=1, source_target_pairs={{0,16},{2,18},{4,20},{6,22},{8,24},{10,26},{12,28},{14,30},{16,0},... | collective-permute-start | bytes 12296 | tf_op jit(solution)/shard_map/ppermute | solution.py:473
  39.1 14.3 %collective-permute-start.7 = (f32[8,4096]{1,0:T(8,128)S(1)}, f32[8,4096]{1,0:T(8,128)S(1)}, u32[]{:S(2)}, u32[]{:S(2)}) collective-permute-start(f32[8,4096]{1,0:T(8,128)S(1)} %get-tuple-element.28), channel_id=1, source_target_pairs={{0,2},{2,0},{4,6},{6,4},{8,10},{10,8},{12,14},{14,12},{16,18},{18,... | collective-permute-start | bytes 393224 | tf_op jit(solution)/shard_map/ppermute | solution.py:497
  39.2 13.0 %collective-permute-start.5 = (bf16[8,4096]{1,0:T(8,128)(2,1)S(1)}, bf16[8,4096]{1,0:T(8,128)(2,1)S(1)}, u32[]{:S(2)}, u32[]{:S(2)}) collective-permute-start(bf16[8,4096]{1,0:T(8,128)(2,1)S(1)} %get-tuple-element.26), channel_id=1, source_target_pairs={{0,6},{2,4},{4,2},{6,0},{8,14},{10,12},{12,10},{14,8},{16,22},{18,... | collective-permute-start | bytes 196616 | tf_op jit(solution)/shard_map/ppermute | solution.py:497
  49.0 4.4 %collective-permute-start.6 = (bf16[8,4096]{1,0:T(8,128)(2,1)S(1)}, bf16[8,4096]{1,0:T(8,128)(2,1)S(1)}, u32[]{:S(2)}, u32[]{:S(2)}) collective-permute-start(bf16[8,4096]{1,0:T(8,128)(2,1)S(1)} %get-tuple-element.27), channel_id=1, source_target_pairs={{0,4},{2,6},{4,0},{6,2},{8,12},{10,14},{12,8},{14,10},{16,20},{18,... | collective-permute-start | bytes 196616 | tf_op jit(solution)/shard_map/ppermute | solution.py:497
  53.5 3.8 %collective-permute-start.8 = (bf16[8,1024]{1,0:T(8,128)(2,1)S(1)}, bf16[8,1024]{1,0:T(8,128)(2,1)S(1)}, u32[]{:S(2)}, u32[]{:S(2)}) collective-permute-start(bf16[8,1024]{1,0:T(8,128)(2,1)S(1)} %get-tuple-element.31), channel_id=1, source_target_pairs={{0,8},{2,10},{4,12},{6,14},{8,0},{10,2},{12,4},{14,6},{16,24},{18,... | collective-permute-start | bytes 49160 | tf_op jit(solution)/shard_map/ppermute | solution.py:514
  55.4 5.5 %collective-permute-start.10 = (bf16[8,1024]{1,0:T(8,128)(2,1)S(1)}, bf16[8,1024]{1,0:T(8,128)(2,1)S(1)}, u32[]{:S(2)}, u32[]{:S(2)}) collective-permute-start(bf16[8,1024]{1,0:T(8,128)(2,1)S(1)} %get-tuple-element.32), channel_id=1, source_target_pairs={{0,24},{2,26},{4,28},{6,30},{8,16},{10,18},{12,20},{14,22},{16,8},... | collective-permute-start | bytes 49160 | tf_op jit(solution)/shard_map/ppermute | solution.py:514
  56.4 4.9 %collective-permute-start.9 = (bf16[8,1024]{1,0:T(8,128)(2,1)S(1)}, bf16[8,1024]{1,0:T(8,128)(2,1)S(1)}, u32[]{:S(2)}, u32[]{:S(2)}) collective-permute-start(bf16[8,1024]{1,0:T(8,128)(2,1)S(1)} %get-tuple-element.33), channel_id=1, source_target_pairs={{0,16},{2,18},{4,20},{6,22},{8,24},{10,26},{12,28},{14,30},{16,0},... | collective-permute-start | bytes 49160 | tf_op jit(solution)/shard_map/ppermute | solution.py:514

commit v5 on v4

--- a/solution.py
+++ b/solution.py
@@ -54,7 +54,7 @@
 
 
 def chunk_start(me, near, far, chunk):
-    return pl.multiple_of((me ^ (near | (far << 2))) * chunk, chunk)
+    return pl.multiple_of(((far << 2) + ((me & 3) ^ near)) * chunk, chunk)
 
 
 def held_copies(me, inverse_ref, held_refs, near_refs, sems=None):
@@ -177,18 +177,28 @@
     def pairs_step(step_id, carry):
         results = []
         for at in range(UNROLL):
-            live, volume, control = tiles_of((step_id - 2) * UNROLL + at)
-            weight = weights[jnp.where(live, volume, vtiles)]
-            terms = jnp.dot(weight, kernels[at], preferred_element_type=jnp.float32)
-            results.append((control, terms[:ROWS] + terms[ROWS:]))
+            if at % 2 == 0:
+                controls, pair_weights = [], []
+                for slot in ((step_id - 2) * UNROLL + at, (step_id - 2) * UNROLL + at + 1):
+                    live, volume, control = tiles_of(slot)
+                    pair_weights.append(weights[jnp.where(live, volume, vtiles)])
+                    controls.append(control)
+                terms = jnp.dot(
+                    jnp.concatenate(pair_weights, axis=0),
+                    kernels[at // 2],
+                    preferred_element_type=jnp.float32,
+                )
+                results.append((controls[0], terms[:ROWS, :CT] + terms[ROWS : 2 * ROWS, :CT]))
+                results.append((controls[1], terms[2 * ROWS : 3 * ROWS, CT:] + terms[3 * ROWS :, CT:]))
             squared = jnp.maximum(squares[at], 1e-12)
             radius = squared * lax.rsqrt(squared)
             inside = jnp.maximum(4.0 - radius, 0.0)
             inside = inside * inside
             kernel = inside * inside * (radius + 1.0)
             high = kernel.astype(jnp.bfloat16)
-            kernels[at, :VT] = high
-            kernels[at, VT:] = (kernel - high.astype(jnp.float32)).astype(jnp.bfloat16)
+            place = slice((at % 2) * CT, (at % 2 + 1) * CT)
+            kernels[at // 2, :VT, place] = high
+            kernels[at // 2, VT:, place] = (kernel - high.astype(jnp.float32)).astype(jnp.bfloat16)
             _, volume, control = tiles_of(step_id * UNROLL + at)
             squares[at] = jnp.dot(
                 nodes[volume], points[control], preferred_element_type=jnp.float32
@@ -231,7 +241,7 @@
         pltpu.VMEM((vtiles + 1, 2 * ROWS, 2 * VT), jnp.bfloat16),
         pltpu.VMEM((tiles + 1, ROWS, CT), jnp.float32),
         pltpu.VMEM((UNROLL, VT, CT), jnp.float32),
-        pltpu.VMEM((UNROLL, 2 * VT, CT), jnp.bfloat16),
+        pltpu.VMEM((UNROLL // 2, 2 * VT, 2 * CT), jnp.bfloat16),
         pltpu.VMEM(sens.shape, jnp.float32),
         pltpu.VMEM(vol.shape, jnp.float32),
         pltpu.VMEM(ctl.shape, jnp.float32),
@@ -508,12 +518,11 @@
     )
     for part in moved:
         total = total + part.astype(jnp.float32)
-    result = total[:, :chunk]
-    for end in ends[1:]:
-        sent = total[:, end * chunk : (end + 1) * chunk].astype(jnp.bfloat16)
-        got = lax.ppermute(sent, "wide", [(at, at ^ (end << 2)) for at in spans])
-        result = result + got.astype(jnp.float32)
-    return result[:components]
+    total = total.reshape(ROWS, len(ends), chunk).transpose(1, 0, 2)
+    sent = total.astype(jnp.bfloat16)
+    groups = [[(end << 2) + low for end in ends] for low in range(4)]
+    got = lax.all_to_all(sent, "wide", 0, 0, axis_index_groups=groups, tiled=True)
+    return jnp.sum(got.astype(jnp.float32), axis=0)[:components]
 
 
 def solution(mesh):

time: 63 us -> 63.1 us (level); the launches traced: 61.9 us -> 63.4 us
  blocking collectives: 0 us -> 10.6 us
  starting transfers between devices: 22.4 us -> 17.6 us
  waiting for transfers between devices: 9.69 us -> 5.46 us
    all_to_all x0 -> x1, blocking collectives: none -> 10.6 us  [local(): lax.all_to_all(sent, 'wide', 0, 0, axis_index_groups=groups, tiled=True)]
    ppermute x3 -> x0, waiting for transfers between devices: 4.23 us -> none  [local(): got = lax.ppermute(sent, 'wide', [(at, at ^ end << 2) for at in spans])]
    ppermute x3 -> x0, starting transfers between devices: 3.55 us -> none  [local(): got = lax.ppermute(sent, 'wide', [(at, at ^ end << 2) for at in spans])]
    ppermute x3, starting transfers between devices: 10.2 us -> 8.94 us  [local(): lax.ppermute(part, 'wide', [(at, at ^ difference) for at in spans])]
  transfers between devices with their start and end apart: 11 -> 8, of which waited for: 6 -> 3; matrix products, arithmetic and copies ran while one was open for 0% -> 0% of each run, Pallas kernels for 5% -> 4%
where the time goes in v5:
time: 63.1 us; the launch traced here: 63.4 us
  Pallas kernels  28.3 us (45%)
  starting transfers between devices  17.6 us (28%)
  blocking collectives  10.6 us (17%)
  waiting for transfers between devices  5.46 us (9%)
  other arithmetic  0.74 us (1%)
  between operations  0.7 us (1%)
    pallas_call x1, Pallas kernels, pair_stage(): pl.pallas_call(functools.partial(pair_kernel, geometry, held_count, 1 if...  14.8 us
    pallas_call x2, Pallas kernels, product_stage(): pl.pallas_call(kernel, out_shape=outs, in_specs=[smem()] + [vmem()] * (le...  13.6 us
    all_to_all x1, blocking collectives, local(): lax.all_to_all(sent, 'wide', 0, 0, axis_index_groups=groups, tiled=True)  10.6 us
    ppermute x3, starting transfers between devices, local(): lax.ppermute(part, 'wide', [(at, at ^ difference) for at in spans])  8.94 us
    ppermute x1, starting transfers between devices, local(): far_cross = lax.ppermute(far, both, cross[1])  3.54 us
    ppermute x1, starting transfers between devices, local(): partner = lax.ppermute(own, 'narrow', [(0, 1), (1, 0)])  3.03 us
    ppermute x1, waiting for transfers between devices, local(): far_same = lax.ppermute(far, 'wide', [straight[1](at) for at in spans])  2.65 us
    ppermute x1, starting transfers between devices, local(): spill_a = lax.ppermute(spill, both, cross[0])  1.71 us
  transfers between devices with their start and end apart: 8, of which 3 were waited for; matrix products, arithmetic and copies ran while one was open for 0% of the time, Pallas kernels for 4%

profile of v5, /device:TPU:0, one launch (start us, length us, event | category | flops | bytes accessed | tf_op | source)
XLA Modules:
  0.0 63.4 jit_solution(12280388712050572095)
XLA Ops:
  0.7 0.1 pad_add_fusion.place_ref
  0.7 14.8 %pairs.1 = (f32[16,8,128]{2,1,0:T(8,128)S(1)}, f32[8,8,128]{2,1,0:T(8,128)S(1)}, f32[1,8,128]{2,1,0:T(8,128)S(1)}, bf16[256,16384]{1,0:T(8,128)(2,1)S(1)}, bf16[...) custom-call(s32[1]{0:T(128)S(6)} %copy.7.count_ref, ...), custom_call_target="tpu_custom_call" | custom-call | flops 3355443200 | bytes 33554432 | tf_op jit(solution)/shard_map/pairs/pallas_call | solution.py:258
  15.5 3.0 %collective-permute-start = (f32[16,8,128]{2,1,0:T(8,128)S(1)}, f32[16,8,128]{2,1,0:T(8,128)S(1)}, u32[]{:S(2)}, u32[]{:S(2)}) collective-permute-start(f32[16,8,128]{2,1,0:T(8,128)S(1)} %get-tuple-element.17.own_ref), channel_id=1, source_target_pairs={{0,1},{1,0},{2,3},{3,2},{4,5},{5,4},{6,7},{7,6},{8,9},{9,8},{10,11... | collective-permute-start | bytes 196616 | tf_op jit(solution)/shard_map/ppermute | solution.py:469
  18.6 0.0 collective-permute-start.2
  18.6 1.7 %collective-permute-start.1 = (f32[8,8,128]{2,1,0:T(8,128)S(1)}, f32[8,8,128]{2,1,0:T(8,128)S(1)}, u32[]{:S(2)}, u32[]{:S(2)}) collective-permute-start(f32[8,8,128]{2,1,0:T(8,128)S(1)} %get-tuple-element.18), channel_id=1, source_target_pairs={{0,3},{1,2},{2,5},{3,4},{4,7},{5,6},{6,9},{7,8},{8,11},{9,10},{10,... | collective-permute-start | bytes 98312 | tf_op jit(solution)/shard_map/ppermute | solution.py:482
  20.3 3.5 %collective-permute-start.4 = (f32[1,8,128]{2,1,0:T(8,128)S(1)}, f32[1,8,128]{2,1,0:T(8,128)S(1)}, u32[]{:S(2)}, u32[]{:S(2)}) collective-permute-start(f32[1,8,128]{2,1,0:T(8,128)S(1)} %get-tuple-element.19), channel_id=1, source_target_pairs={{0,17},{1,16},{2,19},{3,18},{4,21},{5,20},{6,23},{7,22},{8,25},{9,... | collective-permute-start | bytes 12296 | tf_op jit(solution)/shard_map/ppermute | solution.py:484
  23.8 0.3 collective-permute-start.3
  24.2 1.5 %collective-permute-done.4.far_cross_ref = f32[1,8,128]{2,1,0:T(8,128)S(1)} collective-permute-done((f32[1,8,128]{2,1,0:T(8,128)S(1)}, f32[1,8,128]{2,1,0:T(8,128)S(1)}, u32[]{:S(2)}, u32[]{:S(2)}) %collective-permute-start.4) | collective-permute-done | bytes 4128 | tf_op jit(solution)/shard_map/ppermute | solution.py:484
  25.7 2.6 %collective-permute-done.3.far_same_ref = f32[1,8,128]{2,1,0:T(8,128)S(1)} collective-permute-done((f32[1,8,128]{2,1,0:T(8,128)S(1)}, f32[1,8,128]{2,1,0:T(8,128)S(1)}, u32[]{:S(2)}, u32[]{:S(2)}) %collective-permute-start.3) | collective-permute-done | bytes 4128 | tf_op jit(solution)/shard_map/ppermute | solution.py:483
  28.3 0.0 collective-permute-done.2.spill_b_ref
  28.3 0.0 collective-permute-done.1.spill_a_ref
  28.3 0.0 collective-permute-done.partner_ref
  28.3 10.7 %product_a.1 = (bf16[16,2048]{1,0:T(8,128)(2,1)S(1)}, bf16[8,4096]{1,0:T(8,128)(2,1)S(1)}, bf16[8,4096]{1,0:T(8,128)(2,1)S(1)}, f32[8,4096]{1,0:T(8,128)S(1)}) custom-call(s32[4]{0:T(128)S(1)} %pad_add_fusion.place_ref, f32[16,8,128]{2,1,0:T(8,128)S(1)} %get-tuple-element.17.own_ref, f32[16,8,128]{2,1,0:T(8,128)S(1)} %collective-permute-done.partner_ref, ...), custom_call_target="tpu_custom_call" | custom-call | flops 134217728 | bytes 16777216 | tf_op jit(solution)/shard_map/product_a/pallas_call | solution.py:385
  39.1 0.1 collective-permute-start.7
  39.2 8.5 %collective-permute-start.5 = (bf16[8,4096]{1,0:T(8,128)(2,1)S(1)}, bf16[8,4096]{1,0:T(8,128)(2,1)S(1)}, u32[]{:S(2)}, u32[]{:S(2)}) collective-permute-start(bf16[8,4096]{1,0:T(8,128)(2,1)S(1)} %get-tuple-element.26), channel_id=1, source_target_pairs={{0,6},{2,4},{4,2},{6,0},{8,14},{10,12},{12,10},{14,8},{16,22},{18,... | collective-permute-start | bytes 196616 | tf_op jit(solution)/shard_map/ppermute | solution.py:507
  47.7 0.3 collective-permute-start.6
  48.0 2.8 %product_b.1 = f32[8,4096]{1,0:T(8,128)S(1)} custom-call(s32[4]{0:T(128)S(1)} %pad_add_fusion.place_ref, bf16[16,2048]{1,0:T(8,128)(2,1)S(1)} %get-tuple-element.25.row_loads, bf16[256,16384]{1,0:T(8,128)(2,1)S(1)} %get-tuple-element.20.rest_0_, bf16[256,16384]{1,0:T(8,128)(2,1)S(1)} %get-tuple-element.21.rest_1_, ...), custom_call_target="tpu_custom_call" | custom-call | flops 134217728 | bytes 16777216 | tf_op jit(solution)/shard_map/product_b/pallas_call | solution.py:385
  50.9 0.0 collective-permute-done.5
  50.9 1.3 %collective-permute-done.6 = bf16[8,4096]{1,0:T(8,128)(2,1)S(1)} collective-permute-done((bf16[8,4096]{1,0:T(8,128)(2,1)S(1)}, bf16[8,4096]{1,0:T(8,128)(2,1)S(1)}, u32[]{:S(2)}, u32[]{:S(2)}) %collective-permute-start.6) | collective-permute-done | bytes 65568 | tf_op jit(solution)/shard_map/ppermute | solution.py:507
  52.1 0.0 collective-permute-done.7
  52.2 10.6 %all_to_all.5 = bf16[4,8,1024]{2,1,0:T(8,128)(2,1)S(1)} all-to-all(bf16[4,8,1024]{2,1,0:T(8,128)(2,1)S(1)} %bitcast.8), channel_id=1, replica_groups={{0,8,16,24},{2,10,18,26},{4,12,20,28},{6,14,22,30},{1,9,17,25},{3,11,19..., dimensions={0} | all-to-all | bytes 131072 | tf_op jit(solution)/shard_map/all_to_all | solution.py:524
  62.8 0.6 convert_reduce_fusion
  (1 shorter events, 0.0 us)
Async XLA Ops:
  15.5 12.8 %collective-permute-start = (f32[16,8,128]{2,1,0:T(8,128)S(1)}, f32[16,8,128]{2,1,0:T(8,128)S(1)}, u32[]{:S(2)}, u32[]{:S(2)}) collective-permute-start(f32[16,8,128]{2,1,0:T(8,128)S(1)} %get-tuple-element.17.own_ref), channel_id=1, source_target_pairs={{0,1},{1,0},{2,3},{3,2},{4,5},{5,4},{6,7},{7,6},{8,9},{9,8},{10,11... | collective-permute-start | bytes 196616 | tf_op jit(solution)/shard_map/ppermute | solution.py:469
  18.6 9.8 %collective-permute-start.2 = (f32[8,8,128]{2,1,0:T(8,128)S(1)}, f32[8,8,128]{2,1,0:T(8,128)S(1)}, u32[]{:S(2)}, u32[]{:S(2)}) collective-permute-start(f32[8,8,128]{2,1,0:T(8,128)S(1)} %get-tuple-element.18), channel_id=1, source_target_pairs={{0,2},{2,4},{4,6},{6,8},{8,10},{10,12},{12,14},{14,16},{16,18},{18... | collective-permute-start | bytes 98312 | tf_op jit(solution)/shard_map/ppermute | solution.py:481
  18.6 9.8 %collective-permute-start.1 = (f32[8,8,128]{2,1,0:T(8,128)S(1)}, f32[8,8,128]{2,1,0:T(8,128)S(1)}, u32[]{:S(2)}, u32[]{:S(2)}) collective-permute-start(f32[8,8,128]{2,1,0:T(8,128)S(1)} %get-tuple-element.18), channel_id=1, source_target_pairs={{0,3},{1,2},{2,5},{3,4},{4,7},{5,6},{6,9},{7,8},{8,11},{9,10},{10,... | collective-permute-start | bytes 98312 | tf_op jit(solution)/shard_map/ppermute | solution.py:482
  20.3 5.4 %collective-permute-start.4 = (f32[1,8,128]{2,1,0:T(8,128)S(1)}, f32[1,8,128]{2,1,0:T(8,128)S(1)}, u32[]{:S(2)}, u32[]{:S(2)}) collective-permute-start(f32[1,8,128]{2,1,0:T(8,128)S(1)} %get-tuple-element.19), channel_id=1, source_target_pairs={{0,17},{1,16},{2,19},{3,18},{4,21},{5,20},{6,23},{7,22},{8,25},{9,... | collective-permute-start | bytes 12296 | tf_op jit(solution)/shard_map/ppermute | solution.py:484
  23.8 4.5 %collective-permute-start.3 = (f32[1,8,128]{2,1,0:T(8,128)S(1)}, f32[1,8,128]{2,1,0:T(8,128)S(1)}, u32[]{:S(2)}, u32[]{:S(2)}) collective-permute-start(f32[1,8,128]{2,1,0:T(8,128)S(1)} %get-tuple-element.19), channel_id=1, source_target_pairs={{0,16},{2,18},{4,20},{6,22},{8,24},{10,26},{12,28},{14,30},{16,0},... | collective-permute-start | bytes 12296 | tf_op jit(solution)/shard_map/ppermute | solution.py:483
  39.1 13.0 %collective-permute-start.7 = (f32[8,4096]{1,0:T(8,128)S(1)}, f32[8,4096]{1,0:T(8,128)S(1)}, u32[]{:S(2)}, u32[]{:S(2)}) collective-permute-start(f32[8,4096]{1,0:T(8,128)S(1)} %get-tuple-element.28), channel_id=1, source_target_pairs={{0,2},{2,0},{4,6},{6,4},{8,10},{10,8},{12,14},{14,12},{16,18},{18,... | collective-permute-start | bytes 393224 | tf_op jit(solution)/shard_map/ppermute | solution.py:507
  39.2 11.7 %collective-permute-start.5 = (bf16[8,4096]{1,0:T(8,128)(2,1)S(1)}, bf16[8,4096]{1,0:T(8,128)(2,1)S(1)}, u32[]{:S(2)}, u32[]{:S(2)}) collective-permute-start(bf16[8,4096]{1,0:T(8,128)(2,1)S(1)} %get-tuple-element.26), channel_id=1, source_target_pairs={{0,6},{2,4},{4,2},{6,0},{8,14},{10,12},{12,10},{14,8},{16,22},{18,... | collective-permute-start | bytes 196616 | tf_op jit(solution)/shard_map/ppermute | solution.py:507
  47.7 4.4 %collective-permute-start.6 = (bf16[8,4096]{1,0:T(8,128)(2,1)S(1)}, bf16[8,4096]{1,0:T(8,128)(2,1)S(1)}, u32[]{:S(2)}, u32[]{:S(2)}) collective-permute-start(bf16[8,4096]{1,0:T(8,128)(2,1)S(1)} %get-tuple-element.27), channel_id=1, source_target_pairs={{0,4},{2,6},{4,0},{6,2},{8,12},{10,14},{12,8},{14,10},{16,20},{18,... | collective-permute-start | bytes 196616 | tf_op jit(solution)/shard_map/ppermute | solution.py:507
